TPU v7x, 32 devices: a whole 2x2x4 slice. The times are simulated.
32 devices in a mesh: gx: 8 (over z, core), gy: 4 (over y, x).
Axes of the slice: x: 2, y: 2, z: 4, core: 2. Of those that a mesh axis runs over, the one named last changes fastest.
Arguments:
- mean_field: float32 [128, 256, 128], P('gx', 'gy'), may hold values from -3 to 3
- log_scale: float32 [128, 256, 128], P('gx', 'gy'), may hold values from -2.5 to -0.7
- noise: float32 [128, 256, 128], P('gx', 'gy'), may hold values from -6 to 6
- wave_prev: float32 [128, 256, 128], P('gx', 'gy'), may hold values from -6 to 6
- wave_now: float32 [128, 256, 128], P('gx', 'gy'), may hold values from -6 to 6
- adjoint_next: float32 [128, 256, 128], P('gx', 'gy'), may hold values from -6 to 6
- adjoint_now: float32 [128, 256, 128], P('gx', 'gy'), may hold values from -6 to 6
- sources: int32 [16, 3], replicated, may hold values from 0 to 255, as said below
- receivers: int32 [256, 3], replicated, may hold values from 0 to 255, as said below
- observed: float32 [256], replicated, may hold values from -6 to 6
- step_index: int32 [1], replicated, may hold values from 0 to 47
- prior_scale: float32 [1], replicated, may hold values from 0.5 to 2
Outputs:
- wave_next: float32 [128, 256, 128], P('gx', 'gy')
- adjoint_prev: float32 [128, 256, 128], P('gx', 'gy')
- search: float32 [128, 256, 128], P('gx', 'gy')
- logscale_grad: float32 [128, 256, 128], P('gx', 'gy')
Inputs may be any that keep to these rules, and one draw needn't show every extreme that they name: `sources`: each row gives the first, second and depth cell of a point, below 128, 256 and 128; points may coincide. `receivers`: each row gives the first, second and depth cell of a point, below 128, 256 and 128; points may coincide.
All inputs are finite; a program needn't handle non-finite values.
Results may differ from a plain program's by a relative error of at most 0.000075.
Values sent between devices are 32-bit elements; how exact they have to be, the bound alone decides.
A program may use at most 64 MiB of HBM per device.

v0:
```python
import math

import jax
import jax.numpy as jnp
from jax import lax
from jax.sharding import PartitionSpec as P

NSTEPS = 48


STENCIL_WEIGHTS = (-205.0 / 72.0, 8.0 / 5.0, -1.0 / 5.0, 8.0 / 315.0, -1.0 / 560.0)
COURANT_SQUARED = 0.08
VELOCITY_GAIN = 0.2
PULSE_FREQUENCY = 0.05
PULSE_AMPLITUDE = 20.0


def padded_2(block, sides, width):
    for axis, dim in sides:
        count = lax.axis_size(axis)
        forward = [(i, i + 1) for i in range(count - 1)]
        backward = [(target, source) for source, target in forward]
        low = lax.ppermute(
            lax.slice_in_dim(block, block.shape[dim] - width, None, axis=dim), axis, forward
        )
        high = lax.ppermute(lax.slice_in_dim(block, 0, width, axis=dim), axis, backward)
        block = jnp.concatenate([low, block, high], axis=dim)
    return block


def contract(formula, left, right):
    return jnp.einsum(
        formula, left, right, precision=lax.Precision.HIGHEST, preferred_element_type=jnp.float32
    )


def shifted(padded, dimension, offset):
    result = padded
    for axis_number in range(3):
        anchor = 4 + offset if axis_number == dimension else 4
        length = padded.shape[axis_number + 1] - 8
        result = lax.slice_in_dim(result, anchor, anchor + length, axis=axis_number + 1)
    return result


def laplacian(rimmed):
    padded = jnp.pad(rimmed, ((0, 0), (0, 0), (0, 0), (4, 4)))
    summed = 3.0 * STENCIL_WEIGHTS[0] * shifted(padded, 0, 0)
    for offset in range(1, 5):
        for dimension in range(3):
            summed = summed + STENCIL_WEIGHTS[offset] * (
                shifted(padded, dimension, offset) + shifted(padded, dimension, -offset)
            )
    return summed


def selectors(points, anchor_x, anchor_y, block_x, block_y, depth):
    across = (points[:, 0:1] - anchor_x == lax.iota(jnp.int32, block_x)[None, :]).astype(
        jnp.float32
    )
    lateral = (points[:, 1:2] - anchor_y == lax.iota(jnp.int32, block_y)[None, :]).astype(
        jnp.float32
    )
    levels = (points[:, 2:3] == lax.iota(jnp.int32, depth)[None, :]).astype(jnp.float32)
    columns = (across[:, :, None] * lateral[:, None, :]).reshape(points.shape[0], block_x * block_y)
    return (columns, levels)


def deposit(columns, levels, values):
    return contract("rq,rz->qz", values[:, None] * columns, levels)


def transform_weights(length):
    indices = lax.iota(jnp.int32, length)
    angle = (indices[:, None] * indices[None, :] % length).astype(jnp.float32) * (
        2.0 * math.pi / length
    )
    cosine = jnp.cos(angle)
    sine = jnp.sin(angle)
    return (cosine + sine)[None, None]


def wave_term(waves, length):
    sine = jnp.sin(waves.astype(jnp.float32) * (math.pi / length))
    return (length / 8.0) ** 2 * 4.0 * sine * sine


def spectral_gain(prior_scale, waves_z, waves_y, waves_x, depth, total_y, total_x):
    denominator = (
        1.0 + wave_term(waves_x, total_x) + wave_term(waves_y, total_y) + wave_term(waves_z, depth)
    )
    cells = total_x * total_y * depth
    return prior_scale[0] * (math.sqrt(cells) / 8.0 / cells) / denominator


def prior_smooth(data_grad, prior_scale):
    block_x, block_y, depth = data_grad.shape
    parts_x = lax.axis_size("gx")
    parts_y = lax.axis_size("gy")
    index_x = lax.axis_index("gx")
    index_y = lax.axis_index("gy")
    total_x = block_x * parts_x
    total_y = block_y * parts_y
    components = 1
    flattened = data_grad.reshape(1, block_x * block_y, depth)
    forward_z = transform_weights(depth)
    spectra = contract("qpnk,pan->qka", forward_z, flattened)
    depth_share = depth // parts_y
    width_share = total_y // parts_x
    stacked = spectra.reshape(components, parts_y, depth_share, block_x * block_y)
    stacked = lax.all_to_all(stacked, "gy", split_axis=1, concat_axis=1, tiled=True)
    stacked = stacked.reshape(components, parts_y, depth_share, block_x, block_y)
    weights_y = transform_weights(total_y).reshape(
        components, components, parts_y, block_y, parts_x, width_share
    )
    stacked = contract("qpsybj,pskxy->qbkxj", weights_y, stacked).reshape(
        components, parts_x, depth_share, block_x * width_share
    )
    stacked = lax.all_to_all(stacked, "gx", split_axis=1, concat_axis=1, tiled=True)
    stacked = stacked.reshape(components, parts_x, depth_share, block_x, width_share)
    weights_x = transform_weights(total_x).reshape(
        components, components, parts_x, block_x, total_x
    )
    stacked = contract("qpsxm,pskxj->qkjm", weights_x, stacked)
    waves_z = (index_y * depth_share + lax.iota(jnp.int32, depth_share))[:, None, None]
    waves_y = (index_x * width_share + lax.iota(jnp.int32, width_share))[None, :, None]
    waves_x = lax.iota(jnp.int32, total_x)[None, None, :]
    stacked = (
        stacked
        * spectral_gain(prior_scale, waves_z, waves_y, waves_x, depth, total_y, total_x)[None]
    )
    inverse_x = transform_weights(total_x).reshape(
        components, components, total_x, parts_x, block_x
    )
    stacked = contract("qpmsx,pkjm->qskxj", inverse_x, stacked).reshape(
        components, parts_x, depth_share, block_x * width_share
    )
    stacked = lax.all_to_all(stacked, "gx", split_axis=1, concat_axis=1, tiled=True)
    stacked = stacked.reshape(components, parts_x, depth_share, block_x, width_share)
    inverse_y = transform_weights(total_y).reshape(
        components, components, parts_x, width_share, parts_y, block_y
    )
    stacked = contract("qpbjsy,pbkxj->qskxy", inverse_y, stacked).reshape(
        components, parts_y, depth_share, block_x * block_y
    )
    stacked = lax.all_to_all(stacked, "gy", split_axis=1, concat_axis=1, tiled=True)
    inverse_z = transform_weights(depth).reshape(1, components, parts_y, depth_share, depth)
    result = contract("qpskz,pska->qaz", inverse_z, stacked)
    return result.reshape(block_x, block_y, depth)


def per_device(
    mean_field,
    log_scale,
    noise,
    wave_prev,
    wave_now,
    adjoint_next,
    adjoint_now,
    sources,
    receivers,
    observed,
    step_index,
    prior_scale,
):
    block_x, block_y, depth = wave_now.shape
    anchor_x = lax.axis_index("gx") * block_x
    anchor_y = lax.axis_index("gy") * block_y
    spread = jnp.exp(log_scale)
    sample = mean_field + spread * noise
    speed = COURANT_SQUARED * jnp.exp(2.0 * VELOCITY_GAIN * sample)
    rimmed = padded_2(jnp.stack([wave_now, speed * adjoint_now]), (("gx", 1), ("gy", 2)), 4)
    curves = laplacian(rimmed)
    curved = curves[0]
    moment = (step_index[0] - NSTEPS // 2).astype(jnp.float32) * (math.pi * PULSE_FREQUENCY)
    pulse = PULSE_AMPLITUDE * (1.0 - 2.0 * moment * moment) * jnp.exp(-moment * moment)
    source_columns, source_levels = selectors(sources, anchor_x, anchor_y, block_x, block_y, depth)
    pulses = jnp.ones((sources.shape[0],), jnp.float32) * pulse
    wave_next = 2.0 * wave_now - wave_prev + speed * curved
    wave_next = wave_next + deposit(source_columns, source_levels, pulses).reshape(
        block_x, block_y, depth
    )
    record_columns, record_levels = selectors(
        receivers, anchor_x, anchor_y, block_x, block_y, depth
    )
    traces = contract("qz,rz->rq", wave_next.reshape(block_x * block_y, depth), record_levels)
    picked = jnp.sum(traces * record_columns, axis=1)
    misfit = picked - observed
    adjoint_prev = 2.0 * adjoint_now - adjoint_next + curves[1]
    adjoint_prev = adjoint_prev + deposit(record_columns, record_levels, misfit).reshape(
        block_x, block_y, depth
    )
    data_grad = 2.0 * VELOCITY_GAIN * speed * adjoint_prev * curved
    search = prior_smooth(data_grad, prior_scale) + sample
    logscale_grad = data_grad * spread * noise - 1.0
    return (wave_next, adjoint_prev, search, logscale_grad)


def solution(mesh):
    return jax.shard_map(
        per_device,
        mesh=mesh,
        in_specs=(
            P("gx", "gy", None),
            P("gx", "gy", None),
            P("gx", "gy", None),
            P("gx", "gy", None),
            P("gx", "gy", None),
            P("gx", "gy", None),
            P("gx", "gy", None),
            P(),
            P(),
            P(),
            P(),
            P(),
        ),
        out_specs=(
            P("gx", "gy", None),
            P("gx", "gy", None),
            P("gx", "gy", None),
            P("gx", "gy", None),
        ),
        check_vma=False,
    )
```

profile of v0, /device:TPU:0, one launch (start us, length us, event | category | flops | bytes accessed | tf_op | source)
XLA Modules:
  0.0 121.3 jit_solution(13643346403974029821)
XLA Ops:
  0.7 1.8 %multiply_bitcast_fusion = (f32[1,16,64,128]{3,2,1,0:T(8,128)S(1)}, f32[16,64,128]{2,1,0:T(8,128)S(1)}) fusion(f32[16,64,128]{2,1,0:T(8,128)} %param.18, f32[16,64,128]{2,1,0:T(8,128)} %param.12, f32[16,64,128]{2,1,0:T(8,128)} %param.14, f32[16,64,128]{2,1,0:T(8,128)} %param.13), kind=kLoop, calls=%fused_computation.102 | loop fusion | flops 655360 | bytes 3145728 | tf_op jit(solution)/shard_map/stack | solution.py:172
  2.5 0.8 fusion.61
  3.3 1.3 %collective-permute-start = (f32[2,4,64,128]{3,2,1,0:T(8,128)}, f32[2,4,64,128]{3,2,1,0:T(8,128)S(1)}, u32[]{:S(2)}, u32[]{:S(2)}) collective-permute-start(f32[2,4,64,128]{3,2,1,0:T(8,128)} %get-tuple-element.15), channel_id=1, source_target_pairs={{4,0},{8,4},{12,8},{16,12},{20,16},{24,20},{28,24},{5,1},{9,5},{13... | collective-permute-start | bytes 786440 | tf_op jit(solution)/shard_map/ppermute | solution.py:26
  4.6 3.0 %collective-permute-start.1 = (f32[2,4,64,128]{3,2,1,0:T(8,128)}, f32[2,4,64,128]{3,2,1,0:T(8,128)S(1)}, u32[]{:S(2)}, u32[]{:S(2)}) collective-permute-start(f32[2,4,64,128]{3,2,1,0:T(8,128)} %get-tuple-element.14), channel_id=1, source_target_pairs={{0,4},{4,8},{8,12},{12,16},{16,20},{20,24},{24,28},{1,5},{5,9},{9,... | collective-permute-start | bytes 786440 | tf_op jit(solution)/shard_map/ppermute | solution.py:23
  7.7 0.1 fusion.141
  7.8 0.1 fusion.142
  8.6 0.1 broadcast_multiply_fusion.1
  8.7 0.1 multiply_multiply_fusion.1
  8.8 0.1 mul.518
  8.9 0.1 dot_general.48
  9.0 1.3 %copy.37 = f32[256,1024]{1,0:T(8,128)} copy(f32[256,1024]{0,1:T(8,128)S(1)} %bitcast.144) | data formatting | bytes 2097152 | tf_op jit(solution)/shard_map/mul | solution.py:65
  10.3 0.1 mul.533
  10.4 0.3 sine_add_fusion
  10.8 0.0 collective-permute-done
  10.8 0.0 collective-permute-done.1
  10.8 1.3 %collective-permute-start.2 = (f32[2,24,4,128]{3,2,1,0:T(4,128)S(1)}, f32[2,24,4,128]{3,2,1,0:T(4,128)S(1)}, u32[]{:S(2)}, u32[]{:S(2)}) collective-permute-start(f32[2,24,4,128]{3,2,1,0:T(4,128)S(1)} %get-tuple-element.11), channel_id=1, source_target_pairs={{1,0},{2,1},{3,2},{5,4},{6,5},{7,6},{9,8},{10,9},{11,10},{13,12},{... | collective-permute-start | bytes 294920 | tf_op jit(solution)/shard_map/ppermute | solution.py:26
  12.1 5.5 %collective-permute-start.3 = (f32[2,24,4,128]{3,2,1,0:T(4,128)S(1)}, f32[2,24,4,128]{3,2,1,0:T(4,128)S(1)}, u32[]{:S(2)}, u32[]{:S(2)}) collective-permute-start(f32[2,24,4,128]{3,2,1,0:T(4,128)S(1)} %get-tuple-element.10), channel_id=1, source_target_pairs={{0,1},{1,2},{2,3},{4,5},{5,6},{6,7},{8,9},{9,10},{10,11},{12,13},{... | collective-permute-start | bytes 294920 | tf_op jit(solution)/shard_map/ppermute | solution.py:23
  17.6 0.3 pad_maximum_fusion.2
  18.0 0.3 collective-permute-done.2
  18.3 1.6 %collective-permute-done.3 = f32[2,24,4,128]{3,2,1,0:T(4,128)S(1)} collective-permute-done((f32[2,24,4,128]{3,2,1,0:T(4,128)S(1)}, f32[2,24,4,128]{3,2,1,0:T(4,128)S(1)}, u32[]{:S(2)}, u32[]{:S(2)}) %collective-permute-start.3) | collective-permute-done | bytes 98336 | tf_op jit(solution)/shard_map/ppermute | solution.py:23
  19.9 0.3 pad_maximum_fusion
  20.2 3.3 %select_maximum_fusion = f32[2,24,72,136]{3,2,1,0:T(8,128)S(1)} fusion(f32[2,24,4,128]{3,2,1,0:T(4,128)S(1)} %collective-permute-done.2, f32[2,24,4,128]{3,2,1,0:T(4,128)S(1)} %collective-permute-done.3, f32[2,4,64,128]{3,2,1,0:T(8,128)S(1)} %collective-permute-done, f32[2,4,64,128]{3,2,1,0:T(8,128)S(1)} %collective-permute-done.1, ...), kind=kLoop, calls=%fused_computation.2 | loop fusion | flops 6580224 | bytes 3649536 | tf_op jit(solution)/shard_map/concatenate | solution.py:27
  23.5 0.0 copy-start.7
  23.5 2.5 %fusion.22 = f32[2,16,64,128]{3,2,1,0:T(8,128)S(1)} fusion(f32[1,16,64,128]{3,2,1,0:T(8,128)S(1)} %get-tuple-element.6, f32[1,16,64,128]{3,2,1,0:T(8,128)S(1)} %bitcast.143, f32[2,24,72,136]{3,2,1,0:T(8,128)S(1)} %select_maximum_fusion, f32[2,24,68,128]{3,2,1,0:T(8,128)S(1)} %get-tuple-element.9, f32[2,24,68,128]{3,2,1,0:T(8,128)S(1)} %get-tuple-element.8, ...), kind=kLoop, calls=%fused_computation.44 | loop fusion | flops 9961472 | bytes 27262976 | tf_op jit(solution)/shard_map/add | solution.py:51
  26.0 0.0 copy-start.1
  26.0 0.0 copy-done.7
  26.0 0.0 copy-start.10
  26.1 0.6 convolution_add_fusion
  26.7 0.0 copy-start.5
  26.7 0.0 copy-start.2
  26.7 0.0 copy-start.3
  26.7 0.0 copy-start.4
  26.7 0.0 copy-start.6
  26.8 0.5 copy-done.1
  27.2 0.7 fusion.6
  28.0 0.1 broadcast_multiply_fusion
  28.1 0.0 copy-done.2
  28.1 0.1 copy-done.3
  28.2 0.2 copy-done.4
  28.3 0.2 copy-done.6
  28.5 1.8 %multiply_add_fusion = (f32[16,64,128]{2,1,0:T(8,128)}, f32[16,64,128]{2,1,0:T(8,128)S(1)}, f32[16,64,128]{2,1,0:T(8,128)}) fusion(f32[16,64,128]{2,1,0:T(8,128)S(1)} %copy-done.3, f32[16,64,128]{2,1,0:T(8,128)S(1)} %copy-done.4, f32[2,16,64,128]{3,2,1,0:T(8,128)S(1)} %fusion.22, f32[16,64,128]{2,1,0:T(8,128)S(1)} %get-tuple-element.7, ...), kind=kOutput, calls=%fused_computation.92 | convolution fusion | flops 404127744 | bytes 6292480 | tf_op jit(solution)/shard_map/rq,rz->qz/dot_general | solution.py:32
  30.3 1.4 %convolution_bitcast_fusion.3 = f32[1,4,32,1024]{3,2,0,1:T(8,128)} fusion(f32[4,32,128]{2,1,0:T(8,128)S(1)} %bitcast.154, f32[1024,128,1]{1,0,2:T(8,128)S(1)} %bitcast.148), kind=kOutput, calls=%fused_computation.28 | convolution fusion | flops 201326592 | bytes 1114112 | tf_op jit(solution)/shard_map/qpnk,pan->qka/dot_general | solution.py:32
  31.7 6.7 %all-to-all-start = ((f32[1,4,32,1024]{3,2,0,1:T(8,128)}), f32[1,4,32,1024]{3,2,0,1:T(8,128)S(1)}, u32[]{:S(2)}, u32[]{:S(2)}) async-start(f32[1,4,32,1024]{3,2,0,1:T(8,128)} %convolution_bitcast_fusion.3), calls=%async_computation | async-start | bytes 1048576 | tf_op jit(solution)/shard_map/all_to_all | solution.py:111
  38.4 9.2 %all-to-all-done = f32[1,4,32,1024]{3,2,0,1:T(8,128)S(1)} async-done(((f32[1,4,32,1024]{3,2,0,1:T(8,128)}), f32[1,4,32,1024]{3,2,0,1:T(8,128)S(1)}, u32[]{:S(2)}, u32[]{:S(2)}) %all-to-all-start) | async-done | bytes 524320 | tf_op jit(solution)/shard_map/all_to_all | solution.py:111
  47.5 0.3 reshape.441
  47.8 5.6 %convolution_bitcast_fusion = f32[1,8,32,16,32]{4,2,1,3,0:T(8,128)S(1)} fusion(f32[4,32,16,64,1]{3,2,1,0,4:T(8,128)S(1)} %bitcast.152, s32[8,32]{1,0:T(8,128)S(1)} %multiply_add_fusion.3, s32[4,64]{1,0:T(4,128)S(1)} %multiply_add_fusion.4), kind=kOutput, calls=%fused_computation.12 | convolution fusion | flops 403636224 | bytes 1050624 | tf_op jit(solution)/shard_map/qpsybj,pskxy->qbkxj/dot_general | solution.py:32
  53.4 1.2 copy.40
  54.6 1.6 %reshape.442 = f32[1,8,32,512]{3,2,1,0:T(8,128)} reshape(f32[1,8,32,16,32]{4,3,2,1,0:T(8,128)S(1)} %copy.40) | data formatting | bytes 1048576 | tf_op jit(solution)/shard_map/reshape | solution.py:116
  56.2 4.2 %all-to-all-start.1 = ((f32[1,8,32,512]{3,2,0,1:T(8,128)}), f32[1,8,32,512]{3,2,0,1:T(8,128)S(1)}, u32[]{:S(2)}, u32[]{:S(2)}) async-start(f32[1,8,32,512]{3,2,0,1:T(8,128)} %bitcast.147), calls=%async_computation.1 | async-start | bytes 1048576 | tf_op jit(solution)/shard_map/all_to_all | solution.py:119
  61.3 0.1 broadcast_add_fusion
  61.3 14.5 %all-to-all-done.1 = f32[1,8,32,512]{3,2,0,1:T(8,128)S(1)} async-done(((f32[1,8,32,512]{3,2,0,1:T(8,128)}), f32[1,8,32,512]{3,2,0,1:T(8,128)S(1)}, u32[]{:S(2)}, u32[]{:S(2)}) %all-to-all-start.1) | async-done | bytes 524320 | tf_op jit(solution)/shard_map/all_to_all | solution.py:119
  75.8 0.5 reshape.443
  76.4 3.6 %fusion.8 = f32[32,32,128,1]{2,1,3,0:T(8,128)S(1)} fusion(f32[8,32,16,32]{3,2,1,0:T(8,128)S(1)} %reshape.443, f32[32]{0:T(128)S(1)} %multiply_multiply_fusion.2, f32[32,128]{1,0:T(8,128)S(1)} %broadcast_add_fusion, f32[]{:T(128)} %bitcast.35, s32[8,16]{1,0:T(8,128)S(1)} %multiply_add_fusion.2), kind=kOutput, calls=%fused_computation.27 | convolution fusion | flops 201965568 | bytes 1065604 | tf_op jit(solution)/shard_map/qpsxm,pskxj->qkjm/dot_general | solution.py:32
  80.0 2.5 %convolution_bitcast_fusion.1 = f32[1,8,32,16,32]{4,3,1,2,0:T(8,128)S(1)} fusion(f32[32,32,128,1]{2,1,3,0:T(8,128)S(1)} %fusion.8, s32[8,16]{1,0:T(8,128)S(1)} %multiply_add_fusion.2), kind=kOutput, calls=%fused_computation.13 | convolution fusion | flops 201572352 | bytes 1049088 | tf_op jit(solution)/shard_map/qpmsx,pkjm->qskxj/dot_general | solution.py:32
  82.4 0.8 reshape.444
  83.3 0.3 copy.42
  83.6 17.8 %all_to_all.20 = f32[1,8,32,512]{3,2,0,1:T(8,128)S(1)} all-to-all(f32[1,8,32,512]{3,2,0,1:T(8,128)S(1)} %copy.42), channel_id=1, replica_groups=mesh['gx'=8,'gy'=4] {'gx'}, dimensions={1} | all-to-all | bytes 1048576 | tf_op jit(solution)/shard_map/all_to_all | solution.py:138
  101.4 0.5 reshape.445
  101.9 4.4 %fusion.3 = f32[1,4,32,16,64]{4,2,1,3,0:T(8,128)S(1)} fusion(f32[8,32,16,32,1]{3,2,1,0,4:T(8,128)S(1)} %bitcast.146, s32[4,64]{1,0:T(4,128)S(1)} %multiply_add_fusion.4, s32[8,32]{1,0:T(8,128)S(1)} %multiply_add_fusion.3), kind=kOutput, calls=%fused_computation.19 | convolution fusion | flops 403636224 | bytes 1050624 | tf_op jit(solution)/shard_map/qpbjsy,pbkxj->qskxy/dot_general | solution.py:32
  106.3 0.6 copy.44
  106.9 0.3 reshape.446
  107.2 10.8 %all_to_all.21 = f32[1,4,32,1024]{3,2,0,1:T(8,128)S(1)} all-to-all(f32[1,4,32,1024]{3,2,0,1:T(8,128)S(1)} %bitcast.149), channel_id=1, replica_groups=mesh['gx'=8,'gy'=4] {'gy'}, dimensions={1} | all-to-all | bytes 1048576 | tf_op jit(solution)/shard_map/all_to_all | solution.py:146
  118.1 0.3 dot_general.64
  118.4 2.9 %fusion.9 = f32[16,64,128]{2,1,0:T(8,128)} fusion(f32[16,64,128]{2,1,0:T(8,128)S(1)} %get-tuple-element.7, f32[16,64,32,4]{1,0,2,3:T(8,128)S(1)} %dot_general.64, s32[4,32]{1,0:T(4,128)S(1)} %multiply_add_fusion.5), kind=kOutput, calls=%fused_computation.31 | convolution fusion | flops 201703424 | bytes 1573376 | tf_op jit(solution)/shard_map/qpskz,pska->qaz/dot_general | solution.py:32
  (21 shorter events, 0.3 us)
Async XLA Ops:
  0.6 1.9 %copy-start = (f32[16,64,128]{2,1,0:T(8,128)S(1)}, f32[16,64,128]{2,1,0:T(8,128)}, u32[]{:S(2)}) copy-start(f32[16,64,128]{2,1,0:T(8,128)} %param.16) | copy-start | bytes 1572868
  0.6 7.0 %copy-start.9 = (s32[16,3]{0,1:T(4,128)S(1)}, s32[16,3]{0,1:T(4,128)}, u32[]{:S(2)}) copy-start(s32[16,3]{0,1:T(4,128)} %param.19) | copy-start | bytes 580
  0.7 7.9 %copy-start.8 = (s32[256,3]{0,1:T(4,128)S(1)}, s32[256,3]{0,1:T(4,128)}, u32[]{:S(2)}) copy-start(s32[256,3]{0,1:T(4,128)} %param.20) | copy-start | bytes 9220
  3.3 7.5 %collective-permute-start = (f32[2,4,64,128]{3,2,1,0:T(8,128)}, f32[2,4,64,128]{3,2,1,0:T(8,128)S(1)}, u32[]{:S(2)}, u32[]{:S(2)}) collective-permute-start(f32[2,4,64,128]{3,2,1,0:T(8,128)} %get-tuple-element.15), channel_id=1, source_target_pairs={{4,0},{8,4},{12,8},{16,12},{20,16},{24,20},{28,24},{5,1},{9,5},{13... | collective-permute-start | bytes 786440 | tf_op jit(solution)/shard_map/ppermute | solution.py:26
  4.6 6.2 %collective-permute-start.1 = (f32[2,4,64,128]{3,2,1,0:T(8,128)}, f32[2,4,64,128]{3,2,1,0:T(8,128)S(1)}, u32[]{:S(2)}, u32[]{:S(2)}) collective-permute-start(f32[2,4,64,128]{3,2,1,0:T(8,128)} %get-tuple-element.14), channel_id=1, source_target_pairs={{0,4},{4,8},{8,12},{12,16},{16,20},{20,24},{24,28},{1,5},{5,9},{9,... | collective-permute-start | bytes 786440 | tf_op jit(solution)/shard_map/ppermute | solution.py:23
  10.8 7.4 %collective-permute-start.2 = (f32[2,24,4,128]{3,2,1,0:T(4,128)S(1)}, f32[2,24,4,128]{3,2,1,0:T(4,128)S(1)}, u32[]{:S(2)}, u32[]{:S(2)}) collective-permute-start(f32[2,24,4,128]{3,2,1,0:T(4,128)S(1)} %get-tuple-element.11), channel_id=1, source_target_pairs={{1,0},{2,1},{3,2},{5,4},{6,5},{7,6},{9,8},{10,9},{11,10},{13,12},{... | collective-permute-start | bytes 294920 | tf_op jit(solution)/shard_map/ppermute | solution.py:26
  12.1 7.7 %collective-permute-start.3 = (f32[2,24,4,128]{3,2,1,0:T(4,128)S(1)}, f32[2,24,4,128]{3,2,1,0:T(4,128)S(1)}, u32[]{:S(2)}, u32[]{:S(2)}) collective-permute-start(f32[2,24,4,128]{3,2,1,0:T(4,128)S(1)} %get-tuple-element.10), channel_id=1, source_target_pairs={{0,1},{1,2},{2,3},{4,5},{5,6},{6,7},{8,9},{9,10},{10,11},{12,13},{... | collective-permute-start | bytes 294920 | tf_op jit(solution)/shard_map/ppermute | solution.py:23
  23.5 2.5 %copy-start.7 = (f32[16,64,128]{2,1,0:T(8,128)S(1)}, f32[16,64,128]{2,1,0:T(8,128)}, u32[]{:S(2)}) copy-start(f32[16,64,128]{2,1,0:T(8,128)} %param.15) | copy-start | bytes 1572868
  26.0 1.2 %copy-start.1 = (f32[256,1024]{1,0:T(8,128)S(1)}, f32[256,1024]{1,0:T(8,128)}, u32[]{:S(2)}) copy-start(f32[256,1024]{1,0:T(8,128)} %copy.37) | copy-start | bytes 3145732
  26.0 2.0 %copy-start.10 = (f32[256]{0:T(256)S(1)}, f32[256]{0:T(256)}, u32[]{:S(2)}) copy-start(f32[256]{0:T(256)} %param.21) | copy-start | bytes 3076
  26.7 3.6 %copy-start.5 = (f32[16,64,128]{2,1,0:T(8,128)}, f32[16,64,128]{2,1,0:T(8,128)S(1)}, u32[]{:S(2)}) copy-start(f32[16,64,128]{2,1,0:T(8,128)S(1)} %convolution_add_fusion) | copy-start | bytes 1572868
  26.7 1.4 %copy-start.2 = (f32[16,64,128]{2,1,0:T(8,128)S(1)}, f32[16,64,128]{2,1,0:T(8,128)}, u32[]{:S(2)}) copy-start(f32[16,64,128]{2,1,0:T(8,128)} %param.18) | copy-start | bytes 1572868
  26.7 1.5 %copy-start.3 = (f32[16,64,128]{2,1,0:T(8,128)S(1)}, f32[16,64,128]{2,1,0:T(8,128)}, u32[]{:S(2)}) copy-start(f32[16,64,128]{2,1,0:T(8,128)} %param.14) | copy-start | bytes 1572868
  26.7 1.6 %copy-start.4 = (f32[16,64,128]{2,1,0:T(8,128)S(1)}, f32[16,64,128]{2,1,0:T(8,128)}, u32[]{:S(2)}) copy-start(f32[16,64,128]{2,1,0:T(8,128)} %param.13) | copy-start | bytes 1572868
  26.7 1.7 %copy-start.6 = (f32[16,64,128]{2,1,0:T(8,128)S(1)}, f32[16,64,128]{2,1,0:T(8,128)}, u32[]{:S(2)}) copy-start(f32[16,64,128]{2,1,0:T(8,128)} %param.17) | copy-start | bytes 1572868
  31.7 15.9 %all-to-all-start = ((f32[1,4,32,1024]{3,2,0,1:T(8,128)}), f32[1,4,32,1024]{3,2,0,1:T(8,128)S(1)}, u32[]{:S(2)}, u32[]{:S(2)}) async-start(f32[1,4,32,1024]{3,2,0,1:T(8,128)} %convolution_bitcast_fusion.3), calls=%async_computation | async-start | bytes 1048576 | tf_op jit(solution)/shard_map/all_to_all | solution.py:111
  56.2 19.6 %all-to-all-start.1 = ((f32[1,8,32,512]{3,2,0,1:T(8,128)}), f32[1,8,32,512]{3,2,0,1:T(8,128)S(1)}, u32[]{:S(2)}, u32[]{:S(2)}) async-start(f32[1,8,32,512]{3,2,0,1:T(8,128)} %bitcast.147), calls=%async_computation.1 | async-start | bytes 1048576 | tf_op jit(solution)/shard_map/all_to_all | solution.py:119
where the time goes:
time: 122 us; the launch traced here: 121 us
  blocking collectives  28.6 us (23%)
  waiting for transfers between devices  25.6 us (21%)
  matrix products  23.5 us (19%)
  starting transfers between devices  22 us (18%)
  other arithmetic  10.1 us (8%)
  local copies, waits for them, and re-layouts  8.99 us (7%)
  between operations  2.41 us (2%)
    dot_general x9, matrix products, contract(): jnp.einsum(formula, left, right, precision=lax.Precision.HIGHEST, preferr...  23.5 us
    all_to_all x1, blocking collectives, prior_smooth(): lax.all_to_all(stacked, 'gx', split_axis=1, concat_axis=1, tiled=True)  17.8 us
    all_to_all x1, waiting for transfers between devices, prior_smooth(): lax.all_to_all(stacked, 'gx', split_axis=1, concat_axis=1, tiled=True)  14.5 us
    all_to_all x1, blocking collectives, prior_smooth(): lax.all_to_all(stacked, 'gy', split_axis=1, concat_axis=1, tiled=True)  10.8 us
    all_to_all x1, waiting for transfers between devices, prior_smooth(): lax.all_to_all(stacked, 'gy', split_axis=1, concat_axis=1, tiled=True)  9.16 us
    ppermute x2, starting transfers between devices, padded_2(): lax.ppermute(lax.slice_in_dim(block, block.shape[dim] - width, None, axis...  8.52 us
    all_to_all x1, starting transfers between devices, prior_smooth(): lax.all_to_all(stacked, 'gy', split_axis=1, concat_axis=1, tiled=True)  6.7 us
    all_to_all x1, starting transfers between devices, prior_smooth(): lax.all_to_all(stacked, 'gx', split_axis=1, concat_axis=1, tiled=True)  4.23 us
  transfers between devices with their start and end apart: 6, of which 4 were waited for; matrix products, arithmetic and copies ran while one was open for 2% of the time, Pallas kernels for 0%

commit v1 on v0

v1 whole, which is shorter than its diff:
```python
import functools
import math

import jax
import jax.numpy as jnp
import ml_dtypes
import numpy as np
from jax import lax
from jax.experimental import pallas as pl
from jax.experimental.pallas import tpu as pltpu
from jax.sharding import PartitionSpec as P

NSTEPS = 48
STENCIL_WEIGHTS = (-205.0 / 72.0, 8.0 / 5.0, -1.0 / 5.0, 8.0 / 315.0, -1.0 / 560.0)
COURANT_SQUARED = 0.08
VELOCITY_GAIN = 0.2
PULSE_FREQUENCY = 0.05
PULSE_AMPLITUDE = 20.0

REACH = 4
PAD = 8
LANES = 128
CHUNKS = 1
MESH = pl.DeviceIdType.MESH
F32 = jnp.float32
BF16 = jnp.bfloat16
NN = (((1,), (0,)), ((), ()))
NT = (((1,), (1,)), ((), ()))


def halves(table):
    high = table.astype(ml_dtypes.bfloat16)
    low = (table - high.astype(np.float64)).astype(ml_dtypes.bfloat16)
    return np.stack([high, low])


def cas(length):
    index = np.arange(length)
    angle = (index[:, None] * index[None, :] % length) * (2.0 * math.pi / length)
    return np.cos(angle) + np.sin(angle)


def wave_term(length):
    return (length / 8.0) ** 2 * 4.0 * np.sin(np.arange(length) * (math.pi / length)) ** 2


def tables(bx, by, nz, nxp, nyp, chunks):
    total_x, total_y = bx * nxp, by * nyp
    along_z = np.zeros((nz, nz))
    for o in range(1, REACH + 1):
        along_z += STENCIL_WEIGHTS[o] * (np.eye(nz, k=o) + np.eye(nz, k=-o))
    face_low = np.zeros((REACH, REACH))
    face_high = np.zeros((REACH, REACH))
    for i in range(REACH):
        for h in range(REACH):
            if h >= i:
                face_low[i, h] = STENCIL_WEIGHTS[i + REACH - h]
            if h <= i:
                face_high[i, h] = STENCIL_WEIGHTS[REACH + h - i]
    faces = np.stack([np.kron(np.eye(bx), face_low), np.kron(np.eye(bx), face_high)])
    pair = LANES // by
    weights_y = cas(total_y).reshape(nyp, by, total_y)
    forward_y = np.zeros((nyp, pair, by, pair, total_y))
    for s in range(pair):
        forward_y[:, s, :, s, :] = weights_y
    forward_y = forward_y.reshape(nyp * LANES, pair * total_y)
    c = (total_x / 8.0) ** 2
    d = 1.0 + wave_term(nz)[:, None] + wave_term(total_y)[None, :]
    log_r = -2.0 * np.arcsinh(0.5 * np.sqrt(d / c))
    r = np.exp(log_r)
    scale = math.sqrt(total_x * total_y * nz) / 8.0 / (nz * total_y)
    scale = scale / (c * -2.0 * np.sinh(log_r))
    closure = 1.0 / -np.expm1(total_x * log_r)
    share = nz // nyp
    sub = share // chunks
    tiles = total_y // LANES
    rows = sub * tiles // nxp
    segment = np.stack([np.exp(bx * log_r), closure])
    segment = segment.reshape(2, nyp, chunks, nxp // tiles, rows, tiles, LANES)
    segment = segment.transpose(1, 2, 3, 5, 0, 4, 6).reshape(nyp, chunks, nxp, 2, rows, LANES)
    as32 = lambda a: np.ascontiguousarray(a).astype(np.float32)
    return (
        as32(along_z),
        as32(faces),
        halves(cas(nz)),
        halves(forward_y),
        halves(forward_y.T),
        as32(np.stack([r, scale]).reshape(2, nyp, share, total_y)),
        as32(segment),
    )


def split(x):
    high = x.astype(BF16)
    return high, (x - high.astype(F32)).astype(BF16)


def split3(x):
    high = x.astype(BF16)
    rest = x - high.astype(F32)
    mid = rest.astype(BF16)
    return high, mid, (rest - mid.astype(F32)).astype(BF16)


def dot(a, b, dims=NN):
    return lax.dot_general(a, b, dims, preferred_element_type=F32)


def dot3(x, w):
    high, low = split(x)
    return dot(high, w[0]) + dot(high, w[1]) + dot(low, w[0])


def exact(a, b):
    return lax.dot_general(a, b, NN, precision=lax.Precision.HIGHEST, preferred_element_type=F32)


def kernel(
    nxp,
    nyp,
    chunks,
    mean_h,
    scale_h,
    noise_h,
    prev_h,
    now_h,
    anext_h,
    anow_h,
    src_row,
    src_col,
    rec_row,
    rec_col,
    observed,
    step,
    prior,
    along_z,
    faces,
    cas_z,
    fwd_y,
    inv_y,
    line_tab,
    seg_tab,
    wave_o,
    adj_o,
    search_o,
    lgrad_o,
    mean,
    logs,
    noise,
    prev,
    anext,
    anow,
    wpad,
    bpad,
    curl,
    acurl,
    speed,
    xrecv,
    ysend,
    yrecv,
    zsend,
    zrecv,
    lines,
    isend,
    irecv,
    msend,
    mrecv,
    rsend,
    rrecv,
    lsem,
    osem,
    xs,
    xr,
    ys,
    yr,
    zs,
    zr,
    ms,
    mr,
    rs,
    rr,
    vs,
    vr,
):
    bx, by, nz = mean.shape
    gx, gy = lax.axis_index("gx"), lax.axis_index("gy")
    pairs = bx * by // LANES
    pair = LANES // by
    share = nz // nyp
    sub = share // chunks
    total_y = by * nyp
    tiles = total_y // LANES
    rows = sub * tiles // nxp
    cells = bx * by
    centre = pl.ds(PAD, by)

    loads = [
        pltpu.make_async_copy(now_h, wpad.at[:, centre, :], lsem.at[0]),
        pltpu.make_async_copy(scale_h, logs, lsem.at[1]),
        pltpu.make_async_copy(noise_h, noise, lsem.at[2]),
        pltpu.make_async_copy(mean_h, mean, lsem.at[3]),
        pltpu.make_async_copy(anow_h, anow, lsem.at[4]),
        pltpu.make_async_copy(prev_h, prev, lsem.at[5]),
        pltpu.make_async_copy(anext_h, anext, lsem.at[6]),
    ]
    for load in loads:
        load.start()

    for padded in (wpad, bpad):
        padded[:, 0:PAD, :] = jnp.zeros((bx, PAD, nz), F32)
        padded[:, PAD + by : by + 2 * PAD, :] = jnp.zeros((bx, PAD, nz), F32)
    outside = ((gx == 0, gx == nxp - 1), (gy == 0, gy == nyp - 1))
    for side in range(2):

        @pl.when(outside[0][side])
        def _():
            for field in range(2):
                xrecv[field, side] = jnp.zeros(xrecv.shape[2:], F32)

        @pl.when(outside[1][side])
        def _():
            for field in range(2):
                yrecv[field, side] = jnp.zeros(yrecv.shape[2:], F32)

    barrier = pltpu.get_barrier_semaphore()
    for i in range(1, nxp):
        pl.semaphore_signal(
            barrier, inc=1, device_id={"gx": lax.rem(gx + i, nxp)}, device_id_type=MESH
        )
    for i in range(1, nyp):
        pl.semaphore_signal(
            barrier, inc=1, device_id={"gy": lax.rem(gy + i, nyp)}, device_id_type=MESH
        )
    pl.semaphore_wait(barrier, nxp + nyp - 2)

    def rim_copy(axis, field, side, src):
        me, count = ((gx, nxp), (gy, nyp))[axis]
        target = lax.rem(me + (1 if side == 0 else count - 1), count)
        land, send, recv = ((xrecv, xs, xr), (yrecv, ys, yr))[axis]
        return pltpu.make_async_remote_copy(
            src_ref=src,
            dst_ref=land.at[field, side],
            send_sem=send.at[field, side],
            recv_sem=recv.at[field, side],
            device_id={("gx", "gy")[axis]: target},
            device_id_type=MESH,
        )

    def start_rim(axis, field, side, src):
        copy = rim_copy(axis, field, side, src)

        @pl.when(jnp.logical_not(outside[axis][1 - side]))
        def _():
            copy.start()

        return (axis, side, copy)

    rims = []
    rims.append(start_rim(0, 0, 0, now_h.at[pl.ds(bx - REACH, REACH)]))
    rims.append(start_rim(0, 0, 1, now_h.at[pl.ds(0, REACH)]))

    def pack_faces(field, padded):
        for x in range(bx):
            here = pl.ds(REACH * x, REACH)
            ysend[field, 0, here, :] = padded[x, PAD + by - REACH : PAD + by, :]
            ysend[field, 1, here, :] = padded[x, PAD : PAD + REACH, :]
        for side in range(2):
            rims.append(start_rim(1, field, side, ysend.at[field, side]))

    loads[0].wait()
    pack_faces(0, wpad)

    for load in loads[1:5]:
        load.wait()

    def pointwise(x):
        turned = jnp.exp(logs[x]) * noise[x]
        sample = mean[x] + turned
        logs[x] = turned
        mean[x] = sample
        fast = COURANT_SQUARED * jnp.exp(2.0 * VELOCITY_GAIN * sample)
        speed[x] = fast
        bpad[x, centre, :] = fast * anow[x]

    for x in range(REACH):
        pointwise(x)
    rims.append(start_rim(0, 1, 1, bpad.at[pl.ds(0, REACH), centre, :]))
    for x in range(bx - REACH, bx):
        pointwise(x)
    rims.append(start_rim(0, 1, 0, bpad.at[pl.ds(bx - REACH, REACH), centre, :]))
    for x in range(REACH, bx - REACH):
        pointwise(x)
    pack_faces(1, bpad)

    def inner_laplacian(padded, out):
        for x0 in range(0, bx, REACH):
            block = padded[x0 : x0 + REACH, PAD : PAD + by, :].reshape(REACH * by, nz)
            depthwise = exact(block, along_z[...]).reshape(REACH, by, nz)
            for x in range(x0, x0 + REACH):
                total = depthwise[x - x0] + 3.0 * STENCIL_WEIGHTS[0] * padded[x, centre, :]
                for o in range(1, REACH + 1):
                    near = padded[x, PAD + o : PAD + o + by, :] + padded[x, PAD - o : PAD - o + by, :]
                    if x + o < bx:
                        near = near + padded[x + o, centre, :]
                    if x - o >= 0:
                        near = near + padded[x - o, centre, :]
                    total = total + STENCIL_WEIGHTS[o] * near
                out[x] = total

    inner_laplacian(wpad, curl)

    def codes(points):
        across = points[0:1, :] - gx * bx
        lateral = points[1:2, :] - gy * by
        inside = (across >= 0) & (across < bx) & (lateral >= 0) & (lateral < by)
        return jnp.where(inside, across * by + lateral, -1)

    src_code = codes(src_row)
    rec_code = codes(rec_row)

    def rim_terms(field, out):
        for side in range(2):
            terms = exact(faces[side], yrecv[field, side])
            first = 0 if side == 0 else by - REACH
            for x in range(bx):
                here = out[x, first : first + REACH, :]
                out[x, first : first + REACH, :] = here + terms[REACH * x : REACH * (x + 1), :]

    def x_rim(field, x):
        total = None
        for o in range(1, REACH + 1):
            if x - o < 0:
                term = STENCIL_WEIGHTS[o] * xrecv[field, 0, REACH + x - o]
                total = term if total is None else total + term
            if x + o >= bx:
                term = STENCIL_WEIGHTS[o] * xrecv[field, 1, x + o - bx]
                total = term if total is None else total + term
        return total

    def wait_rims(field_rims):
        for axis, side, copy in field_rims:

            @pl.when(jnp.logical_not(outside[axis][side]))
            def _():
                copy.wait_recv()

    inner_laplacian(bpad, acurl)
    loads[5].wait()
    loads[6].wait()

    wave_rims = rims[0:4]
    adj_rims = rims[4:8]
    wait_rims(wave_rims)
    rim_terms(0, curl)
    for x in range(bx):
        curved = curl[x]
        extra = x_rim(0, x)
        if extra is not None:
            curved = curved + extra
            curl[x] = curved
        prev[x] = 2.0 * wpad[x, centre, :] - prev[x] + speed[x] * curved

    moment = (step[...] - NSTEPS // 2).astype(F32) * (math.pi * PULSE_FREQUENCY)
    pulse = PULSE_AMPLITUDE * (1.0 - 2.0 * moment * moment) * jnp.exp(-moment * moment)
    nsrc, nrec = src_row.shape[1], rec_row.shape[1]
    src_level = (src_col[:, 2:3] == lax.broadcasted_iota(jnp.int32, (nsrc, nz), 1)).astype(F32)
    src_level = src_level.astype(BF16)
    rec_level = (rec_col[:, 2:3] == lax.broadcasted_iota(jnp.int32, (nrec, nz), 1)).astype(F32)
    rec_level = rec_level.astype(BF16)
    step_x = 4
    block = step_x * by
    picked = jnp.zeros((1, nrec), F32)
    for x0 in range(0, bx, step_x):
        cell = lax.broadcasted_iota(jnp.int32, (block, nsrc), 0) + x0 * by
        hit = (cell == src_code).astype(F32).astype(BF16)
        wave = prev[x0 : x0 + step_x].reshape(block, nz) + pulse * dot(hit, src_level)
        prev[x0 : x0 + step_x] = wave.reshape(step_x, by, nz)
        traces = sum(dot(part, rec_level, NT) for part in split3(wave))
        cell = lax.broadcasted_iota(jnp.int32, (block, nrec), 0) + x0 * by
        picked = picked + jnp.sum(
            jnp.where(cell == rec_code, traces, 0.0), axis=0, keepdims=True
        )
    wave_out = pltpu.make_async_copy(prev, wave_o, osem.at[0])
    wave_out.start()
    misfit = picked - observed[...]

    wait_rims(adj_rims)
    rim_terms(1, acurl)
    misfit_parts = split3(misfit)
    for x0 in range(0, bx, step_x):
        cell = lax.broadcasted_iota(jnp.int32, (block, nrec), 0) + x0 * by
        hit = cell == rec_code
        added = sum(
            dot(jnp.where(hit, part.astype(F32), 0.0).astype(BF16), rec_level)
            for part in misfit_parts
        ).reshape(step_x, by, nz)
        for x in range(x0, x0 + step_x):
            total = acurl[x]
            extra = x_rim(1, x)
            if extra is not None:
                total = total + extra
            adjoint = 2.0 * anow[x] - anext[x] + total + added[x - x0]
            anext[x] = adjoint
            grad = (2.0 * VELOCITY_GAIN) * speed[x] * adjoint * curl[x]
            acurl[x] = grad
            anow[x] = grad * logs[x] - 1.0

        high, low = split(acurl[x0 : x0 + step_x].reshape(block, nz))
        zsend[:, x0 * by : x0 * by + block] = (
            dot(cas_z[0], high, NT) + dot(cas_z[1], high, NT) + dot(cas_z[0], low, NT)
        )

    def z_copy(c, i):
        to = lax.rem(gy + i, nyp)
        return pltpu.make_async_remote_copy(
            src_ref=zsend.at[pl.ds(pl.multiple_of(to * share + c * sub, sub), sub), :],
            dst_ref=zrecv.at[c, gy],
            send_sem=zs.at[c, i],
            recv_sem=zr.at[c, i],
            device_id={"gy": to},
            device_id_type=MESH,
        )

    def own_z(c):
        zrecv[c, gy] = zsend[pl.ds(pl.multiple_of(gy * share + c * sub, sub), sub), :]

    z_copies = [[z_copy(c, i) for i in range(1, nyp)] for c in range(chunks)]
    for c in range(chunks):
        for copy in z_copies[c]:
            copy.start()
    adj_out = pltpu.make_async_copy(anext, adj_o, osem.at[1])
    adj_out.start()
    lgrad_out = pltpu.make_async_copy(anow, lgrad_o, osem.at[2])
    lgrad_out.start()
    for c in range(chunks):
        own_z(c)

    def ratio(c):
        return line_tab[0, gy, c * sub : (c + 1) * sub, :]

    def at(c, x):
        first = (x // pair) * sub
        left = (x % pair) * total_y
        return lines[c, first : first + sub, left : left + total_y]

    def segment(o):
        return (
            slice((o // tiles) * rows, (o // tiles + 1) * rows),
            slice((o % tiles) * LANES, (o % tiles + 1) * LANES),
        )

    def small_copy(src, dst, send, recv, c, i):
        to = lax.rem(gx + i, nxp)
        return pltpu.make_async_remote_copy(
            src_ref=src.at[c, to],
            dst_ref=dst.at[c, gx],
            send_sem=send.at[c, i],
            recv_sem=recv.at[c, i],
            device_id={"gx": to},
            device_id_type=MESH,
        )

    m_copies, r_copies, v_copies = [], [], []

    def lateral(c):
        for copy in z_copies[c]:
            copy.wait_recv()
        block = jnp.concatenate(
            [
                jnp.concatenate(
                    [zrecv[c, p, :, LANES * j : LANES * (j + 1)] for p in range(nyp)], axis=1
                )
                for j in range(pairs)
            ],
            axis=0,
        )
        lines[c] = dot3(block, fwd_y)
        r = ratio(c)
        up = at(c, 0)
        down = at(c, bx - 1)
        for x in range(1, bx):
            up = at(c, x) + r * up
            down = at(c, bx - 1 - x) + r * down
        for o in range(nxp):
            here = segment(o)
            msend[c, o, 0:rows, :] = up[here]
            msend[c, o, rows : 2 * rows, :] = down[here]
        copies = [small_copy(msend, mrecv, ms, mr, c, i) for i in range(1, nxp)]
        for copy in copies:
            copy.start()
        mrecv[c, gx] = msend[c, gx]
        m_copies.append(copies)

    def close(c):
        for copy in m_copies[c]:
            copy.wait_recv()
        decay = seg_tab[gy, c, gx, 0]
        closure = seg_tab[gy, c, gx, 1]
        ups = [mrecv[c, d, 0:rows, :] for d in range(nxp)]
        downs = [mrecv[c, d, rows : 2 * rows, :] for d in range(nxp)]
        up, down = ups[0], downs[nxp - 1]
        for d in range(1, nxp):
            up = ups[d] + decay * up
            down = downs[nxp - 1 - d] + decay * down
        up = up * closure
        down = down * closure
        for d in range(nxp):
            rsend[c, d, 0:rows, :] = up
            up = ups[d] + decay * up
        for d in range(nxp - 1, -1, -1):
            rsend[c, d, rows : 2 * rows, :] = down
            down = downs[d] + decay * down
        copies = [small_copy(rsend, rrecv, rs, rr, c, i) for i in range(1, nxp)]
        for copy in copies:
            copy.start()
        rrecv[c, gx] = rsend[c, gx]
        r_copies.append(copies)

    def back(c):
        for copy in r_copies[c]:
            copy.wait_recv()

        def whole(first):
            return jnp.concatenate(
                [
                    jnp.concatenate(
                        [rrecv[c, i * tiles + t, first : first + rows, :] for t in range(tiles)],
                        axis=1,
                    )
                    for i in range(nxp // tiles)
                ],
                axis=0,
            )

        r = ratio(c)
        gain = line_tab[1, gy, c * sub : (c + 1) * sub, :] * prior[...]
        up, down = whole(0), whole(rows)
        ups = []
        for x in range(bx):
            up = at(c, x) + r * up
            ups.append(up)
        for x in range(bx - 1, -1, -1):
            ahead = r * down
            here = at(c, x)
            down = here + ahead
            first = (x // pair) * sub
            left = (x % pair) * total_y
            lines[c, first : first + sub, left : left + total_y] = gain * (ups[x] + ahead)
        field = dot3(lines[c], inv_y)
        for p in range(nyp):
            isend[c, p] = field[:, LANES * p : LANES * (p + 1)]
        copies = []
        for i in range(1, nyp):
            to = lax.rem(gy + i, nyp)
            copies.append(
                pltpu.make_async_remote_copy(
                    src_ref=isend.at[c, to],
                    dst_ref=irecv.at[c, gy],
                    send_sem=vs.at[c, i],
                    recv_sem=vr.at[c, i],
                    device_id={"gy": to},
                    device_id_type=MESH,
                )
            )
        for copy in copies:
            copy.start()
        irecv[c, gy] = isend[c, gy]
        v_copies.append(copies)

    for stage in range(chunks + 2):
        if stage >= 2:
            back(stage - 2)
        if 1 <= stage <= chunks:
            close(stage - 1)
        if stage < chunks:
            lateral(stage)

    for c in range(chunks):
        for copy in v_copies[c]:
            copy.wait_recv()
    for j in range(pairs):
        spectrum = jnp.concatenate(
            [irecv[c, p, sub * j : sub * (j + 1), :] for p in range(nyp) for c in range(chunks)],
            axis=0,
        )
        smooth = dot3(spectrum.T, cas_z).reshape(pair, by, nz)
        for s in range(pair):
            x = pair * j + s
            mean[x] = mean[x] + smooth[s]
    search_out = pltpu.make_async_copy(mean, search_o, osem.at[3])
    search_out.start()

    for axis, side, copy in rims:

        @pl.when(jnp.logical_not(outside[axis][1 - side]))
        def _():
            copy.wait_send()

    for group in (z_copies, m_copies, r_copies, v_copies):
        for copies in group:
            for copy in copies:
                copy.wait_send()
    wave_out.wait()
    adj_out.wait()
    lgrad_out.wait()
    search_out.wait()


def per_device(
    nxp,
    nyp,
    mean_field,
    log_scale,
    noise,
    wave_prev,
    wave_now,
    adjoint_next,
    adjoint_now,
    sources,
    receivers,
    observed,
    step_index,
    prior_scale,
):
    bx, by, nz = wave_now.shape
    chunks = CHUNKS
    constants = tables(bx, by, nz, nxp, nyp, chunks)
    pairs = bx * by // LANES
    share = nz // nyp
    sub = share // chunks
    total_y = by * nyp
    rows = sub * (total_y // LANES) // nxp
    field = jax.ShapeDtypeStruct((bx, by, nz), F32)
    vmem = pl.BlockSpec(memory_space=pltpu.VMEM)
    hbm = pl.BlockSpec(memory_space=pl.ANY)
    dma = pltpu.SemaphoreType.DMA
    whole = pltpu.VMEM((bx, by, nz), F32)
    padded = pltpu.VMEM((bx, by + 2 * PAD, nz), F32)
    scratch = [whole] * 6 + [padded] * 2 + [whole] * 3
    scratch += [
        pltpu.VMEM((2, 2, REACH, by, nz), F32),
        pltpu.VMEM((2, 2, REACH * bx, nz), F32),
        pltpu.VMEM((2, 2, REACH * bx, nz), F32),
        pltpu.VMEM((nz, bx * by), F32),
        pltpu.VMEM((chunks, nyp, sub, bx * by), F32),
        pltpu.VMEM((chunks, pairs * sub, nyp * LANES), F32),
        pltpu.VMEM((chunks, nyp, pairs * sub, LANES), F32),
        pltpu.VMEM((chunks, nyp, pairs * sub, LANES), F32),
        pltpu.VMEM((chunks, nxp, 2 * rows, LANES), F32),
        pltpu.VMEM((chunks, nxp, 2 * rows, LANES), F32),
        pltpu.VMEM((chunks, nxp, 2 * rows, LANES), F32),
        pltpu.VMEM((chunks, nxp, 2 * rows, LANES), F32),
        dma((7,)),
        dma((4,)),
        dma((2, 2)),
        dma((2, 2)),
        dma((2, 2)),
        dma((2, 2)),
    ]
    scratch += [dma((chunks, nyp))] * 2 + [dma((chunks, nxp))] * 4 + [dma((chunks, nyp))] * 2
    filled = (-sources.shape[0]) % LANES
    src = jnp.pad(sources, ((0, filled), (0, 0)), constant_values=-1)
    return pl.pallas_call(
        functools.partial(kernel, nxp, nyp, chunks),
        out_shape=(field,) * 4,
        in_specs=[hbm] * 7 + [vmem] * (7 + len(constants)),
        out_specs=(hbm,) * 4,
        scratch_shapes=scratch,
        compiler_params=pltpu.CompilerParams(
            collective_id=0, has_side_effects=True, vmem_limit_bytes=50 * 2**20
        ),
    )(
        mean_field,
        log_scale,
        noise,
        wave_prev,
        wave_now,
        adjoint_next,
        adjoint_now,
        src.T,
        src,
        receivers.T,
        receivers,
        observed.reshape(1, -1),
        step_index.reshape(1, 1),
        prior_scale.reshape(1, 1),
        *[jnp.asarray(table) for table in constants],
    )


def solution(mesh):
    grid = P("gx", "gy", None)
    return jax.shard_map(
        functools.partial(per_device, mesh.shape["gx"], mesh.shape["gy"]),
        mesh=mesh,
        in_specs=(grid,) * 7 + (P(),) * 5,
        out_specs=(grid,) * 4,
        check_vma=False,
    )
```

time: 122 us -> 51.3 us (0.42)
  Pallas kernels: 0 us -> 39.2 us
  blocking collectives: 28.6 us -> 0 us
  waiting for transfers between devices: 25.6 us -> 0 us
  matrix products: 23.5 us -> 0 us
  starting transfers between devices: 22 us -> 0 us
  other arithmetic: 10.1 us -> 0 us
    pallas_call x0 -> x1, Pallas kernels: none -> 39.2 us  [per_device(): pl.pallas_call(functools.partial(kernel, nxp, nyp, chunks), out_shape=(fi...]
    all_to_all x2 -> x0, blocking collectives: 28.6 us -> none  [the longest x1 17.8 us: prior_smooth(): lax.all_to_all(stacked, 'gx', split_axis=1, concat_axis=1, tiled=True)]
    all_to_all x2 -> x0, waiting for transfers between devices: 23.6 us -> none  [the longest x1 14.5 us: prior_smooth(): lax.all_to_all(stacked, 'gx', split_axis=1, concat_axis=1, tiled=True)]
    dot_general x9 -> x0, matrix products: 23.5 us -> none  [contract(): jnp.einsum(formula, left, right, precision=lax.Precision.HIGHEST, preferr...]
    ppermute x4 -> x0, starting transfers between devices: 11.1 us -> none  [the longest x2 8.52 us: padded_2(): lax.ppermute(lax.slice_in_dim(block, block.shape[dim] - width, None, axis...]
    all_to_all x2 -> x0, starting transfers between devices: 10.9 us -> none  [the longest x1 6.7 us: prior_smooth(): lax.all_to_all(stacked, 'gy', split_axis=1, concat_axis=1, tiled=True)]
    unnamed x22 -> x24, local copies, waits for them, and re-layouts: 0.93 us -> 9.55 us
    concatenate x4 -> x0, other arithmetic: 3.97 us -> none  [padded_2(): block = jnp.concatenate([low, block, high], axis=dim)]
  transfers between devices with their start and end apart: 6 -> 0, of which waited for: 4 -> 0; matrix products, arithmetic and copies ran while one was open for 2% -> 0% of each run, Pallas kernels for 0% -> 0%
where the time goes in v1:
time: 51.3 us; the launch traced here: 50.9 us
  Pallas kernels  39.2 us (76%)
  local copies, waits for them, and re-layouts  9.63 us (19%)
  between operations  2.05 us (4%)
    pallas_call x1, Pallas kernels, per_device(): pl.pallas_call(functools.partial(kernel, nxp, nyp, chunks), out_shape=(fi...  39.2 us
    unnamed x24, local copies, waits for them, and re-layouts  9.55 us

profile of v1, /device:TPU:0, one launch (start us, length us, event | category | flops | bytes accessed | tf_op | source)
XLA Modules:
  0.0 50.9 jit_solution(3916631622458990866)
XLA Ops:
  0.6 0.0 copy-start.2
  2.0 0.8 %copy.23 = s32[16,3]{1,0:T(8,128)S(1)} copy(s32[16,3]{0,1:T(4,128)} %param.26) | data formatting | bytes 384 | tf_op args[7]
  2.8 0.1 copy.24.src_row
  2.8 0.0 copy-start.4
  2.8 0.0 copy-start.7
  2.8 0.0 copy-start.8
  2.8 0.9 %copy.25.rec_col = s32[256,3]{1,0:T(8,128)S(1)} copy(s32[256,3]{0,1:T(4,128)} %param.27) | data formatting | bytes 6144 | tf_op args[8]
  3.7 0.0 copy-done.2
  3.7 0.0 copy-done.4
  3.8 0.0 copy-done.7
  3.8 0.0 copy-done.8
  3.8 0.0 copy-start
  3.8 1.0 %copy-done = f32[16,64,128]{2,1,0:T(8,128)S(1)} copy-done((f32[16,64,128]{2,1,0:T(8,128)S(1)}, f32[16,64,128]{2,1,0:T(8,128)}, u32[]{:S(2)}) %copy-start) | copy-done | bytes 524312
  4.8 0.0 copy-start.1
  4.8 1.0 %copy-done.1 = f32[16,64,128]{2,1,0:T(8,128)S(1)} copy-done((f32[16,64,128]{2,1,0:T(8,128)S(1)}, f32[16,64,128]{2,1,0:T(8,128)}, u32[]{:S(2)}) %copy-start.1) | copy-done | bytes 524312
  5.9 0.0 copy-start.3
  5.9 0.9 %copy-done.3 = f32[2,4,32,256]{3,2,1,0:T(8,128)S(1)} copy-done((f32[2,4,32,256]{3,2,1,0:T(8,128)S(1)}, f32[2,4,32,256]{3,2,1,0:T(8,128)}, u32[]{:S(2)}) %copy-start.3) | copy-done | bytes 262168
  6.8 0.0 copy-start.5
  6.8 0.8 %copy-done.5 = f32[2,64,64]{2,1,0:T(8,128)S(1)} copy-done((f32[2,64,64]{2,1,0:T(8,128)S(1)}, f32[2,64,64]{2,1,0:T(8,128)}, u32[]{:S(2)}) %copy-start.5) | copy-done | bytes 32792
  7.7 0.0 copy-start.6
  7.7 0.8 %copy-done.6 = f32[128,128]{1,0:T(8,128)S(1)} copy-done((f32[128,128]{1,0:T(8,128)S(1)}, f32[128,128]{1,0:T(8,128)}, u32[]{:S(2)}) %copy-start.6) | copy-done | bytes 65560
  8.5 39.2 %shard_map.210 = (f32[16,64,128]{2,1,0:T(8,128)S(1)}, f32[16,64,128]{2,1,0:T(8,128)S(1)}, f32[16,64,128]{2,1,0:T(8,128)S(1)}, f32[16,64,128]{2,1,0:T(8,128)S(1)}) custom-call(f32[16,64,128]{2,1,0:T(8,128)S(1)} %copy-done, f32[16,64,128]{2,1,0:T(8,128)S(1)} %copy-done.1, f32[16,64,128]{2,1,0:T(8,128)} %noise_h.1, f32[16,64,128]{2,1,0:T(8,128)} %prev_h.1, ...), custom_call_target="tpu_custom_call" | custom-call | tf_op jit(solution)/shard_map/pallas_call | solution.py:663
  47.7 0.8 %copy.32 = f32[16,64,128]{2,1,0:T(8,128)} copy(f32[16,64,128]{2,1,0:T(8,128)S(1)} %get-tuple-element.10) | data formatting | bytes 1048576
  48.5 0.8 %copy.33 = f32[16,64,128]{2,1,0:T(8,128)} copy(f32[16,64,128]{2,1,0:T(8,128)S(1)} %get-tuple-element.11) | data formatting | bytes 1048576
  49.3 0.8 %copy.34 = f32[16,64,128]{2,1,0:T(8,128)} copy(f32[16,64,128]{2,1,0:T(8,128)S(1)} %get-tuple-element.12) | data formatting | bytes 1048576
  50.1 0.8 %copy.35 = f32[16,64,128]{2,1,0:T(8,128)} copy(f32[16,64,128]{2,1,0:T(8,128)S(1)} %get-tuple-element.13) | data formatting | bytes 1048576
  (1 shorter events, 0.0 us)
Async XLA Ops:
  0.6 3.1 %copy-start.2 = (f32[4,1,8,2,8,128]{5,4,3,2,1,0:T(8,128)S(1)}, f32[4,1,8,2,8,128]{5,4,3,2,1,0:T(8,128)}, u32[]{:S(2)}) copy-start(f32[4,1,8,2,8,128]{5,4,3,2,1,0:T(8,128)} %constant.22.clone.seg_tab) | copy-start | bytes 786436
  2.8 0.9 %copy-start.4 = (bf16[2,128,128]{2,1,0:T(8,128)(2,1)S(1)}, bf16[2,128,128]{2,1,0:T(8,128)(2,1)}, u32[]{:S(2)}) copy-start(bf16[2,128,128]{2,1,0:T(8,128)(2,1)} %constant.18.clone.cas_z) | copy-start | bytes 196612
  2.8 0.9 %copy-start.7 = (s32[256,3]{0,1:T(4,128)S(1)}, s32[256,3]{0,1:T(4,128)}, u32[]{:S(2)}) copy-start(s32[256,3]{0,1:T(4,128)} %param.27) | copy-start | bytes 9220
  2.8 0.9 %copy-start.8 = (f32[256]{0:T(256)S(1)}, f32[256]{0:T(256)}, u32[]{:S(2)}) copy-start(f32[256]{0:T(256)} %param.28) | copy-start | bytes 3076
  3.8 1.0 %copy-start = (f32[16,64,128]{2,1,0:T(8,128)S(1)}, f32[16,64,128]{2,1,0:T(8,128)}, u32[]{:S(2)}) copy-start(f32[16,64,128]{2,1,0:T(8,128)} %mean_h.1) | copy-start | bytes 1572868
  4.8 1.0 %copy-start.1 = (f32[16,64,128]{2,1,0:T(8,128)S(1)}, f32[16,64,128]{2,1,0:T(8,128)}, u32[]{:S(2)}) copy-start(f32[16,64,128]{2,1,0:T(8,128)} %scale_h.1) | copy-start | bytes 1572868
  5.9 0.9 %copy-start.3 = (f32[2,4,32,256]{3,2,1,0:T(8,128)S(1)}, f32[2,4,32,256]{3,2,1,0:T(8,128)}, u32[]{:S(2)}) copy-start(f32[2,4,32,256]{3,2,1,0:T(8,128)} %constant.21.clone.line_tab) | copy-start | bytes 786436
  6.8 0.8 %copy-start.5 = (f32[2,64,64]{2,1,0:T(8,128)S(1)}, f32[2,64,64]{2,1,0:T(8,128)}, u32[]{:S(2)}) copy-start(f32[2,64,64]{2,1,0:T(8,128)} %constant.17.clone.faces) | copy-start | bytes 98308
  7.7 0.8 %copy-start.6 = (f32[128,128]{1,0:T(8,128)S(1)}, f32[128,128]{1,0:T(8,128)}, u32[]{:S(2)}) copy-start(f32[128,128]{1,0:T(8,128)} %constant.16.clone.along_z) | copy-start | bytes 196612

commit v2 on v1

--- a/solution.py
+++ b/solution.py
@@ -20,7 +20,8 @@
 REACH = 4
 PAD = 8
 LANES = 128
-CHUNKS = 1
+CHUNKS = 2
+SMALL = 12
 MESH = pl.DeviceIdType.MESH
 F32 = jnp.float32
 BF16 = jnp.bfloat16
@@ -126,62 +127,53 @@
     now_h,
     anext_h,
     anow_h,
-    src_row,
-    src_col,
-    rec_row,
-    rec_col,
-    observed,
-    step,
-    prior,
-    along_z,
-    faces,
-    cas_z,
-    fwd_y,
-    inv_y,
-    line_tab,
-    seg_tab,
-    wave_o,
-    adj_o,
-    search_o,
-    lgrad_o,
-    mean,
-    logs,
-    noise,
-    prev,
-    anext,
-    anow,
-    wpad,
-    bpad,
-    curl,
-    acurl,
-    speed,
-    xrecv,
-    ysend,
-    yrecv,
-    zsend,
-    zrecv,
-    lines,
-    isend,
-    irecv,
-    msend,
-    mrecv,
-    rsend,
-    rrecv,
-    lsem,
-    osem,
-    xs,
-    xr,
-    ys,
-    yr,
-    zs,
-    zr,
-    ms,
-    mr,
-    rs,
-    rr,
-    vs,
-    vr,
+    *rest,
 ):
+    small_h, rest = rest[:SMALL], rest[SMALL:]
+    (wave_o, adj_o, sample_o, lgrad_o, irecv), rest = rest[:5], rest[5:]
+    small, rest = rest[:SMALL], rest[SMALL:]
+    (src_row, rec_row, observed, step, prior) = small[:5]
+    (along_z, faces, cas_z, fwd_y, inv_y, line_tab, seg_tab) = small[5:]
+    (
+        mean,
+        logs,
+        noise,
+        prev,
+        anext,
+        anow,
+        wpad,
+        bpad,
+        curl,
+        acurl,
+        speed,
+        xrecv,
+        ysend,
+        yrecv,
+        zsend,
+        zrecv,
+        lines,
+        isend,
+        msend,
+        mrecv,
+        rsend,
+        rrecv,
+        lsem,
+        tsem,
+        osem,
+        xs,
+        xr,
+        ys,
+        yr,
+        zs,
+        zr,
+        ms,
+        mr,
+        rs,
+        rr,
+        vs,
+        vr,
+        vsem,
+    ) = rest
     bx, by, nz = mean.shape
     gx, gy = lax.axis_index("gx"), lax.axis_index("gy")
     pairs = bx * by // LANES
@@ -204,6 +196,11 @@
         pltpu.make_async_copy(anext_h, anext, lsem.at[6]),
     ]
     for load in loads:
+        load.start()
+    small_loads = [
+        pltpu.make_async_copy(small_h[i], small[i], tsem.at[i]) for i in range(SMALL)
+    ]
+    for load in small_loads:
         load.start()
 
     for padded in (wpad, bpad):
@@ -307,6 +304,8 @@
                     total = total + STENCIL_WEIGHTS[o] * near
                 out[x] = total
 
+    for load in small_loads:
+        load.wait()
     inner_laplacian(wpad, curl)
 
     def codes(points):
@@ -363,19 +362,19 @@
     moment = (step[...] - NSTEPS // 2).astype(F32) * (math.pi * PULSE_FREQUENCY)
     pulse = PULSE_AMPLITUDE * (1.0 - 2.0 * moment * moment) * jnp.exp(-moment * moment)
     nsrc, nrec = src_row.shape[1], rec_row.shape[1]
-    src_level = (src_col[:, 2:3] == lax.broadcasted_iota(jnp.int32, (nsrc, nz), 1)).astype(F32)
-    src_level = src_level.astype(BF16)
-    rec_level = (rec_col[:, 2:3] == lax.broadcasted_iota(jnp.int32, (nrec, nz), 1)).astype(F32)
-    rec_level = rec_level.astype(BF16)
+    src_level = lax.broadcasted_iota(jnp.int32, (nz, nsrc), 0) == src_row[2:3, :]
+    src_level = src_level.astype(F32).astype(BF16)
+    rec_level = lax.broadcasted_iota(jnp.int32, (nz, nrec), 0) == rec_row[2:3, :]
+    rec_level = rec_level.astype(F32).astype(BF16)
     step_x = 4
     block = step_x * by
     picked = jnp.zeros((1, nrec), F32)
     for x0 in range(0, bx, step_x):
         cell = lax.broadcasted_iota(jnp.int32, (block, nsrc), 0) + x0 * by
         hit = (cell == src_code).astype(F32).astype(BF16)
-        wave = prev[x0 : x0 + step_x].reshape(block, nz) + pulse * dot(hit, src_level)
+        wave = prev[x0 : x0 + step_x].reshape(block, nz) + pulse * dot(hit, src_level, NT)
         prev[x0 : x0 + step_x] = wave.reshape(step_x, by, nz)
-        traces = sum(dot(part, rec_level, NT) for part in split3(wave))
+        traces = sum(dot(part, rec_level) for part in split3(wave))
         cell = lax.broadcasted_iota(jnp.int32, (block, nrec), 0) + x0 * by
         picked = picked + jnp.sum(
             jnp.where(cell == rec_code, traces, 0.0), axis=0, keepdims=True
@@ -391,7 +390,7 @@
         cell = lax.broadcasted_iota(jnp.int32, (block, nrec), 0) + x0 * by
         hit = cell == rec_code
         added = sum(
-            dot(jnp.where(hit, part.astype(F32), 0.0).astype(BF16), rec_level)
+            dot(jnp.where(hit, part.astype(F32), 0.0).astype(BF16), rec_level, NT)
             for part in misfit_parts
         ).reshape(step_x, by, nz)
         for x in range(x0, x0 + step_x):
@@ -432,6 +431,8 @@
     adj_out.start()
     lgrad_out = pltpu.make_async_copy(anow, lgrad_o, osem.at[2])
     lgrad_out.start()
+    sample_out = pltpu.make_async_copy(mean, sample_o, osem.at[3])
+    sample_out.start()
     for c in range(chunks):
         own_z(c)
 
@@ -460,7 +461,7 @@
             device_id_type=MESH,
         )
 
-    m_copies, r_copies, v_copies = [], [], []
+    m_copies, r_copies, v_copies, own_fields = [], [], [], []
 
     def lateral(c):
         for copy in z_copies[c]:
@@ -564,7 +565,9 @@
             )
         for copy in copies:
             copy.start()
-        irecv[c, gy] = isend[c, gy]
+        own = pltpu.make_async_copy(isend.at[c, gy], irecv.at[c, gy], vsem.at[c])
+        own.start()
+        own_fields.append(own)
         v_copies.append(copies)
 
     for stage in range(chunks + 2):
@@ -578,18 +581,8 @@
     for c in range(chunks):
         for copy in v_copies[c]:
             copy.wait_recv()
-    for j in range(pairs):
-        spectrum = jnp.concatenate(
-            [irecv[c, p, sub * j : sub * (j + 1), :] for p in range(nyp) for c in range(chunks)],
-            axis=0,
-        )
-        smooth = dot3(spectrum.T, cas_z).reshape(pair, by, nz)
-        for s in range(pair):
-            x = pair * j + s
-            mean[x] = mean[x] + smooth[s]
-    search_out = pltpu.make_async_copy(mean, search_o, osem.at[3])
-    search_out.start()
-
+    for own in own_fields:
+        own.wait()
     for axis, side, copy in rims:
 
         @pl.when(jnp.logical_not(outside[axis][1 - side]))
@@ -603,7 +596,58 @@
     wave_out.wait()
     adj_out.wait()
     lgrad_out.wait()
-    search_out.wait()
+    sample_out.wait()
+
+
+def finish(
+    wave,
+    adjoint,
+    sample_h,
+    lgrad,
+    field_h,
+    cas_h,
+    wave_o,
+    adj_o,
+    search_o,
+    lgrad_o,
+    sample,
+    field,
+    cas_z,
+    search,
+    sem,
+    out_sem,
+):
+    bx, by, nz = sample.shape
+    pair = LANES // by
+    pairs = bx // pair
+    chunks, nyp, height, _ = field.shape
+    sub = height // pairs
+    copies = [
+        pltpu.make_async_copy(field_h, field, sem.at[0]),
+        pltpu.make_async_copy(cas_h, cas_z, sem.at[1]),
+        pltpu.make_async_copy(sample_h, sample, sem.at[2]),
+        pltpu.make_async_copy(wave, wave_o, sem.at[3]),
+        pltpu.make_async_copy(adjoint, adj_o, sem.at[4]),
+        pltpu.make_async_copy(lgrad, lgrad_o, sem.at[5]),
+    ]
+    for copy in copies:
+        copy.start()
+    for copy in copies[:3]:
+        copy.wait()
+    outs = []
+    for j in range(pairs):
+        spectrum = jnp.concatenate(
+            [field[c, p, sub * j : sub * (j + 1), :] for p in range(nyp) for c in range(chunks)],
+            axis=0,
+        )
+        smooth = dot3(spectrum.T, cas_z).reshape(pair, by, nz)
+        here = pl.ds(pair * j, pair)
+        search[here] = sample[here] + smooth
+        out = pltpu.make_async_copy(search.at[here], search_o.at[here], out_sem.at[j])
+        out.start()
+        outs.append(out)
+    for copy in copies[3:] + outs:
+        copy.wait()
 
 
 def per_device(
@@ -625,18 +669,26 @@
     bx, by, nz = wave_now.shape
     chunks = CHUNKS
     constants = tables(bx, by, nz, nxp, nyp, chunks)
+    small = [
+        sources.T,
+        receivers.T,
+        observed.reshape(1, -1),
+        step_index.reshape(1, 1),
+        prior_scale.reshape(1, 1),
+    ] + [jnp.asarray(table) for table in constants]
     pairs = bx * by // LANES
     share = nz // nyp
     sub = share // chunks
     total_y = by * nyp
     rows = sub * (total_y // LANES) // nxp
     field = jax.ShapeDtypeStruct((bx, by, nz), F32)
-    vmem = pl.BlockSpec(memory_space=pltpu.VMEM)
-    hbm = pl.BlockSpec(memory_space=pl.ANY)
+    hbm = pl.BlockSpec(memory_space=pltpu.HBM)
+    anywhere = pl.BlockSpec(memory_space=pl.ANY)
     dma = pltpu.SemaphoreType.DMA
     whole = pltpu.VMEM((bx, by, nz), F32)
     padded = pltpu.VMEM((bx, by + 2 * PAD, nz), F32)
-    scratch = [whole] * 6 + [padded] * 2 + [whole] * 3
+    scratch = [pltpu.VMEM(a.shape, a.dtype) for a in small]
+    scratch += [whole] * 6 + [padded] * 2 + [whole] * 3
     scratch += [
         pltpu.VMEM((2, 2, REACH, by, nz), F32),
         pltpu.VMEM((2, 2, REACH * bx, nz), F32),
@@ -645,12 +697,12 @@
         pltpu.VMEM((chunks, nyp, sub, bx * by), F32),
         pltpu.VMEM((chunks, pairs * sub, nyp * LANES), F32),
         pltpu.VMEM((chunks, nyp, pairs * sub, LANES), F32),
-        pltpu.VMEM((chunks, nyp, pairs * sub, LANES), F32),
         pltpu.VMEM((chunks, nxp, 2 * rows, LANES), F32),
         pltpu.VMEM((chunks, nxp, 2 * rows, LANES), F32),
         pltpu.VMEM((chunks, nxp, 2 * rows, LANES), F32),
         pltpu.VMEM((chunks, nxp, 2 * rows, LANES), F32),
         dma((7,)),
+        dma((SMALL,)),
         dma((4,)),
         dma((2, 2)),
         dma((2, 2)),
@@ -658,34 +710,35 @@
         dma((2, 2)),
     ]
     scratch += [dma((chunks, nyp))] * 2 + [dma((chunks, nxp))] * 4 + [dma((chunks, nyp))] * 2
-    filled = (-sources.shape[0]) % LANES
-    src = jnp.pad(sources, ((0, filled), (0, 0)), constant_values=-1)
-    return pl.pallas_call(
+    scratch += [dma((chunks,))]
+    spread = jax.ShapeDtypeStruct((chunks, nyp, pairs * sub, LANES), F32)
+    wave, adjoint, sample, lgrad, spectrum = pl.pallas_call(
         functools.partial(kernel, nxp, nyp, chunks),
-        out_shape=(field,) * 4,
-        in_specs=[hbm] * 7 + [vmem] * (7 + len(constants)),
-        out_specs=(hbm,) * 4,
+        out_shape=(field,) * 4 + (spread,),
+        in_specs=[hbm] * (7 + len(small)),
+        out_specs=(anywhere,) * 5,
         scratch_shapes=scratch,
         compiler_params=pltpu.CompilerParams(
-            collective_id=0, has_side_effects=True, vmem_limit_bytes=50 * 2**20
+            collective_id=0, has_side_effects=True, vmem_limit_bytes=63 * 2**20
         ),
     )(
-        mean_field,
-        log_scale,
-        noise,
-        wave_prev,
-        wave_now,
-        adjoint_next,
-        adjoint_now,
-        src.T,
-        src,
-        receivers.T,
-        receivers,
-        observed.reshape(1, -1),
-        step_index.reshape(1, 1),
-        prior_scale.reshape(1, 1),
-        *[jnp.asarray(table) for table in constants],
+        mean_field, log_scale, noise, wave_prev, wave_now, adjoint_next, adjoint_now, *small
     )
+    return pl.pallas_call(
+        finish,
+        out_shape=(field,) * 4,
+        in_specs=[anywhere] * 5 + [hbm],
+        out_specs=(hbm,) * 4,
+        scratch_shapes=[
+            whole,
+            pltpu.VMEM(spread.shape, F32),
+            pltpu.VMEM((2, nz, nz), BF16),
+            whole,
+            dma((6,)),
+            dma((pairs,)),
+        ],
+        compiler_params=pltpu.CompilerParams(vmem_limit_bytes=63 * 2**20),
+    )(wave, adjoint, sample, lgrad, spectrum, small[7])
 
 
 def solution(mesh):

time: 51.3 us -> 87 us (1.70)
  Pallas kernels: 39.2 us -> 84.9 us
  local copies, waits for them, and re-layouts: 9.63 us -> 0 us
    pallas_call x0 -> x1, Pallas kernels: none -> 48.9 us  [per_device(): pl.pallas_call(finish, out_shape=(field,) * 4, in_specs=[anywhere] * 5 +...]
    unnamed x24 -> x0, local copies, waits for them, and re-layouts: 9.55 us -> none
    pallas_call x1, Pallas kernels: 39.2 us -> 36 us  [per_device(): pl.pallas_call(functools.partial(kernel, nxp, nyp, chunks), out_shape=(fi...]
where the time goes in v2:
time: 87 us; the launch traced here: 86.9 us
  Pallas kernels  84.9 us (98%)
  between operations  1.93 us (2%)
    pallas_call x1, Pallas kernels, per_device(): pl.pallas_call(finish, out_shape=(field,) * 4, in_specs=[anywhere] * 5 +...  48.9 us
    pallas_call x1, Pallas kernels, per_device(): pl.pallas_call(functools.partial(kernel, nxp, nyp, chunks), out_shape=(fi...  36 us

profile of v2, /device:TPU:0, one launch (start us, length us, event | category | flops | bytes accessed | tf_op | source)
XLA Modules:
  0.0 86.9 jit_solution(3858581089767187739)
XLA Ops:
  1.9 36.0 %shard_map.210 = (f32[16,64,128]{2,1,0:T(8,128)}, f32[16,64,128]{2,1,0:T(8,128)}, f32[16,64,128]{2,1,0:T(8,128)}, f32[16,64,128]{2,1,0:T(8,128)}, f32[2,4,128,128]{3,2,1,0:T(8,128)}) custom-call(f32[16,64,128]{2,1,0:T(8,128)} %mean_h.1, f32[16,64,128]{2,1,0:T(8,128)} %scale_h.1, f32[16,64,128]{2,1,0:T(8,128)} %noise_h.1, f32[16,64,128]{2,1,0:T(8,128)} %prev_h.1, ...), custom_call_target="tpu_custom_call" | custom-call | tf_op jit(solution)/shard_map/pallas_call | solution.py:715
  38.0 48.9 %shard_map.211 = (f32[16,64,128]{2,1,0:T(8,128)}, f32[16,64,128]{2,1,0:T(8,128)}, f32[16,64,128]{2,1,0:T(8,128)}, f32[16,64,128]{2,1,0:T(8,128)}) custom-call(f32[16,64,128]{2,1,0:T(8,128)} %get-tuple-element.9.wave, f32[16,64,128]{2,1,0:T(8,128)} %get-tuple-element.10.adjoint, f32[16,64,128]{2,1,0:T(8,128)} %get-tuple-element.11.sample_h, ...), custom_call_target="tpu_custom_call" | custom-call | tf_op jit(solution)/shard_map/pallas_call | solution.py:727

commit v3 on v2

--- a/solution.py
+++ b/solution.py
@@ -386,6 +386,30 @@
     wait_rims(adj_rims)
     rim_terms(1, acurl)
     misfit_parts = split3(misfit)
+
+    parts = bx // step_x
+
+    def z_copy(c, i, part):
+        to = lax.rem(gy + i, nyp)
+        first = pl.multiple_of(to * share + c * sub, sub)
+        across = pl.ds(0, cells) if part is None else pl.ds(part * block, block)
+        slot = 0 if part is None else part
+        return pltpu.make_async_remote_copy(
+            src_ref=zsend.at[pl.ds(first, sub), across],
+            dst_ref=zrecv.at[c, gy, :, across],
+            send_sem=zs.at[c, slot, i],
+            recv_sem=zr.at[c, slot, i],
+            device_id={"gy": to},
+            device_id_type=MESH,
+        )
+
+    def own_z(c):
+        zrecv[c, gy] = zsend[pl.ds(pl.multiple_of(gy * share + c * sub, sub), sub), :]
+
+    z_copies = [
+        [z_copy(c, i, part) for part in (range(parts) if c == 0 else (None,)) for i in range(1, nyp)]
+        for c in range(chunks)
+    ]
     for x0 in range(0, bx, step_x):
         cell = lax.broadcasted_iota(jnp.int32, (block, nrec), 0) + x0 * by
         hit = cell == rec_code
@@ -408,25 +432,14 @@
         zsend[:, x0 * by : x0 * by + block] = (
             dot(cas_z[0], high, NT) + dot(cas_z[1], high, NT) + dot(cas_z[0], low, NT)
         )
-
-    def z_copy(c, i):
-        to = lax.rem(gy + i, nyp)
-        return pltpu.make_async_remote_copy(
-            src_ref=zsend.at[pl.ds(pl.multiple_of(to * share + c * sub, sub), sub), :],
-            dst_ref=zrecv.at[c, gy],
-            send_sem=zs.at[c, i],
-            recv_sem=zr.at[c, i],
-            device_id={"gy": to},
-            device_id_type=MESH,
-        )
-
-    def own_z(c):
-        zrecv[c, gy] = zsend[pl.ds(pl.multiple_of(gy * share + c * sub, sub), sub), :]
-
-    z_copies = [[z_copy(c, i) for i in range(1, nyp)] for c in range(chunks)]
-    for c in range(chunks):
-        for copy in z_copies[c]:
+        part = x0 // step_x
+        for copy in z_copies[0][part * (nyp - 1) : (part + 1) * (nyp - 1)]:
             copy.start()
+
+    for copies in z_copies[1:]:
+        for copy in copies:
+            copy.start()
+
     adj_out = pltpu.make_async_copy(anext, adj_o, osem.at[1])
     adj_out.start()
     lgrad_out = pltpu.make_async_copy(anow, lgrad_o, osem.at[2])
@@ -614,6 +627,7 @@
     field,
     cas_z,
     search,
+    kept,
     sem,
     out_sem,
 ):
@@ -626,15 +640,20 @@
         pltpu.make_async_copy(field_h, field, sem.at[0]),
         pltpu.make_async_copy(cas_h, cas_z, sem.at[1]),
         pltpu.make_async_copy(sample_h, sample, sem.at[2]),
-        pltpu.make_async_copy(wave, wave_o, sem.at[3]),
-        pltpu.make_async_copy(adjoint, adj_o, sem.at[4]),
-        pltpu.make_async_copy(lgrad, lgrad_o, sem.at[5]),
+        pltpu.make_async_copy(wave, kept.at[0], sem.at[3]),
+        pltpu.make_async_copy(adjoint, kept.at[1], sem.at[4]),
+        pltpu.make_async_copy(lgrad, kept.at[2], sem.at[5]),
     ]
-    for copy in copies:
+    for copy in copies[3:] + copies[:3]:
         copy.start()
+    outs = []
+    for i, kept_o in enumerate((wave_o, adj_o, lgrad_o)):
+        copies[3 + i].wait()
+        out = pltpu.make_async_copy(kept.at[i], kept_o, out_sem.at[pairs + i])
+        out.start()
+        outs.append(out)
     for copy in copies[:3]:
         copy.wait()
-    outs = []
     for j in range(pairs):
         spectrum = jnp.concatenate(
             [field[c, p, sub * j : sub * (j + 1), :] for p in range(nyp) for c in range(chunks)],
@@ -646,8 +665,8 @@
         out = pltpu.make_async_copy(search.at[here], search_o.at[here], out_sem.at[j])
         out.start()
         outs.append(out)
-    for copy in copies[3:] + outs:
-        copy.wait()
+    for out in outs:
+        out.wait()
 
 
 def per_device(
@@ -709,7 +728,7 @@
         dma((2, 2)),
         dma((2, 2)),
     ]
-    scratch += [dma((chunks, nyp))] * 2 + [dma((chunks, nxp))] * 4 + [dma((chunks, nyp))] * 2
+    scratch += [dma((chunks, bx // 4, nyp))] * 2 + [dma((chunks, nxp))] * 4 + [dma((chunks, nyp))] * 2
     scratch += [dma((chunks,))]
     spread = jax.ShapeDtypeStruct((chunks, nyp, pairs * sub, LANES), F32)
     wave, adjoint, sample, lgrad, spectrum = pl.pallas_call(
@@ -734,8 +753,9 @@
             pltpu.VMEM(spread.shape, F32),
             pltpu.VMEM((2, nz, nz), BF16),
             whole,
+            pltpu.VMEM((3, bx, by, nz), F32),
             dma((6,)),
-            dma((pairs,)),
+            dma((pairs + 3,)),
         ],
         compiler_params=pltpu.CompilerParams(vmem_limit_bytes=63 * 2**20),
     )(wave, adjoint, sample, lgrad, spectrum, small[7])

time: 87 us -> 40.3 us (0.46)
  Pallas kernels: 84.9 us -> 38.2 us
    pallas_call x1, Pallas kernels: 48.9 us -> 2.93 us  [per_device(): pl.pallas_call(finish, out_shape=(field,) * 4, in_specs=[anywhere] * 5 +...]
where the time goes in v3:
time: 40.3 us; the launch traced here: 40.1 us
  Pallas kernels  38.2 us (95%)
  between operations  1.93 us (5%)
    pallas_call x1, Pallas kernels, per_device(): pl.pallas_call(functools.partial(kernel, nxp, nyp, chunks), out_shape=(fi...  35.2 us
    pallas_call x1, Pallas kernels, per_device(): pl.pallas_call(finish, out_shape=(field,) * 4, in_specs=[anywhere] * 5 +...  2.93 us

profile of v3, /device:TPU:0, one launch (start us, length us, event | category | flops | bytes accessed | tf_op | source)
XLA Modules:
  0.0 40.1 jit_solution(5778929867073128524)
XLA Ops:
  1.9 35.2 %shard_map.210 = (f32[16,64,128]{2,1,0:T(8,128)}, f32[16,64,128]{2,1,0:T(8,128)}, f32[16,64,128]{2,1,0:T(8,128)}, f32[16,64,128]{2,1,0:T(8,128)}, f32[2,4,128,128]{3,2,1,0:T(8,128)}) custom-call(f32[16,64,128]{2,1,0:T(8,128)} %mean_h.1, f32[16,64,128]{2,1,0:T(8,128)} %scale_h.1, f32[16,64,128]{2,1,0:T(8,128)} %noise_h.1, f32[16,64,128]{2,1,0:T(8,128)} %prev_h.1, ...), custom_call_target="tpu_custom_call" | custom-call | tf_op jit(solution)/shard_map/pallas_call | solution.py:734
  37.2 2.9 %shard_map.211 = (f32[16,64,128]{2,1,0:T(8,128)}, f32[16,64,128]{2,1,0:T(8,128)}, f32[16,64,128]{2,1,0:T(8,128)}, f32[16,64,128]{2,1,0:T(8,128)}) custom-call(f32[16,64,128]{2,1,0:T(8,128)} %get-tuple-element.9.wave, f32[16,64,128]{2,1,0:T(8,128)} %get-tuple-element.10.adjoint, f32[16,64,128]{2,1,0:T(8,128)} %get-tuple-element.11.sample_h, ...), custom_call_target="tpu_custom_call" | custom-call | tf_op jit(solution)/shard_map/pallas_call | solution.py:746

commit v4 on v3

--- a/solution.py
+++ b/solution.py
@@ -20,7 +20,7 @@
 REACH = 4
 PAD = 8
 LANES = 128
-CHUNKS = 2
+CHUNKS = 4
 SMALL = 12
 MESH = pl.DeviceIdType.MESH
 F32 = jnp.float32
@@ -686,7 +686,7 @@
     prior_scale,
 ):
     bx, by, nz = wave_now.shape
-    chunks = CHUNKS
+    chunks = max(1, min(CHUNKS, nz // nyp // 8))
     constants = tables(bx, by, nz, nxp, nyp, chunks)
     small = [
         sources.T,

time: 40.3 us -> 47 us (1.17)
  Pallas kernels: 38.2 us -> 44.9 us
    pallas_call x1, Pallas kernels: 35.2 us -> 42 us  [per_device(): pl.pallas_call(functools.partial(kernel, nxp, nyp, chunks), out_shape=(fi...]
where the time goes in v4:
time: 47 us; the launch traced here: 46.8 us
  Pallas kernels  44.9 us (96%)
  between operations  1.93 us (4%)
    pallas_call x1, Pallas kernels, per_device(): pl.pallas_call(functools.partial(kernel, nxp, nyp, chunks), out_shape=(fi...  42 us
    pallas_call x1, Pallas kernels, per_device(): pl.pallas_call(finish, out_shape=(field,) * 4, in_specs=[anywhere] * 5 +...  2.93 us

profile of v4, /device:TPU:0, one launch (start us, length us, event | category | flops | bytes accessed | tf_op | source)
XLA Modules:
  0.0 46.8 jit_solution(12328412175071904181)
XLA Ops:
  1.9 42.0 %shard_map.210 = (f32[16,64,128]{2,1,0:T(8,128)}, f32[16,64,128]{2,1,0:T(8,128)}, f32[16,64,128]{2,1,0:T(8,128)}, f32[16,64,128]{2,1,0:T(8,128)}, f32[4,4,64,128]{3,2,1,0:T(8,128)}) custom-call(f32[16,64,128]{2,1,0:T(8,128)} %mean_h.1, f32[16,64,128]{2,1,0:T(8,128)} %scale_h.1, f32[16,64,128]{2,1,0:T(8,128)} %noise_h.1, f32[16,64,128]{2,1,0:T(8,128)} %prev_h.1, ...), custom_call_target="tpu_custom_call" | custom-call | tf_op jit(solution)/shard_map/pallas_call | solution.py:734
  43.9 2.9 %shard_map.211 = (f32[16,64,128]{2,1,0:T(8,128)}, f32[16,64,128]{2,1,0:T(8,128)}, f32[16,64,128]{2,1,0:T(8,128)}, f32[16,64,128]{2,1,0:T(8,128)}) custom-call(f32[16,64,128]{2,1,0:T(8,128)} %get-tuple-element.9.wave, f32[16,64,128]{2,1,0:T(8,128)} %get-tuple-element.10.adjoint, f32[16,64,128]{2,1,0:T(8,128)} %get-tuple-element.11.sample_h, ...), custom_call_target="tpu_custom_call" | custom-call | tf_op jit(solution)/shard_map/pallas_call | solution.py:746

commit v5 on v4

--- a/solution.py
+++ b/solution.py
@@ -20,8 +20,8 @@
 REACH = 4
 PAD = 8
 LANES = 128
-CHUNKS = 4
-SMALL = 12
+CHUNKS = 2
+SMALL = 11
 MESH = pl.DeviceIdType.MESH
 F32 = jnp.float32
 BF16 = jnp.bfloat16
@@ -32,7 +32,7 @@
 def halves(table):
     high = table.astype(ml_dtypes.bfloat16)
     low = (table - high.astype(np.float64)).astype(ml_dtypes.bfloat16)
-    return np.stack([high, low])
+    return np.concatenate([high, low, high])
 
 
 def cas(length):
@@ -59,12 +59,6 @@
             if h <= i:
                 face_high[i, h] = STENCIL_WEIGHTS[REACH + h - i]
     faces = np.stack([np.kron(np.eye(bx), face_low), np.kron(np.eye(bx), face_high)])
-    pair = LANES // by
-    weights_y = cas(total_y).reshape(nyp, by, total_y)
-    forward_y = np.zeros((nyp, pair, by, pair, total_y))
-    for s in range(pair):
-        forward_y[:, s, :, s, :] = weights_y
-    forward_y = forward_y.reshape(nyp * LANES, pair * total_y)
     c = (total_x / 8.0) ** 2
     d = 1.0 + wave_term(nz)[:, None] + wave_term(total_y)[None, :]
     log_r = -2.0 * np.arcsinh(0.5 * np.sqrt(d / c))
@@ -84,8 +78,7 @@
         as32(along_z),
         as32(faces),
         halves(cas(nz)),
-        halves(forward_y),
-        halves(forward_y.T),
+        halves(cas(total_y)),
         as32(np.stack([r, scale]).reshape(2, nyp, share, total_y)),
         as32(segment),
     )
@@ -107,9 +100,21 @@
     return lax.dot_general(a, b, dims, preferred_element_type=F32)
 
 
+def parts3(x):
+    high, low = split(x)
+    return jnp.concatenate([high, high, low], axis=1)
+
+
 def dot3(x, w):
-    high, low = split(x)
-    return dot(high, w[0]) + dot(high, w[1]) + dot(low, w[0])
+    return dot(parts3(x), w[...])
+
+
+def trade(left, right):
+    half = LANES // 2
+    low = lax.broadcasted_iota(jnp.int32, left.shape, 1) < half
+    first = jnp.where(low, left, pltpu.roll(right, half, 1))
+    second = jnp.where(low, pltpu.roll(left, half, 1), right)
+    return first, second
 
 
 def exact(a, b):
@@ -133,7 +138,7 @@
     (wave_o, adj_o, sample_o, lgrad_o, irecv), rest = rest[:5], rest[5:]
     small, rest = rest[:SMALL], rest[SMALL:]
     (src_row, rec_row, observed, step, prior) = small[:5]
-    (along_z, faces, cas_z, fwd_y, inv_y, line_tab, seg_tab) = small[5:]
+    (along_z, faces, cas_z, cas_y, line_tab, seg_tab) = small[5:]
     (
         mean,
         logs,
@@ -157,6 +162,7 @@
         mrecv,
         rsend,
         rrecv,
+        hits,
         lsem,
         tsem,
         osem,
@@ -365,7 +371,8 @@
     src_level = lax.broadcasted_iota(jnp.int32, (nz, nsrc), 0) == src_row[2:3, :]
     src_level = src_level.astype(F32).astype(BF16)
     rec_level = lax.broadcasted_iota(jnp.int32, (nz, nrec), 0) == rec_row[2:3, :]
-    rec_level = rec_level.astype(F32).astype(BF16)
+    rec_level = rec_level.astype(F32)
+    level3 = jnp.concatenate([rec_level.astype(BF16)] * 3, axis=0)
     step_x = 4
     block = step_x * by
     picked = jnp.zeros((1, nrec), F32)
@@ -374,10 +381,12 @@
         hit = (cell == src_code).astype(F32).astype(BF16)
         wave = prev[x0 : x0 + step_x].reshape(block, nz) + pulse * dot(hit, src_level, NT)
         prev[x0 : x0 + step_x] = wave.reshape(step_x, by, nz)
-        traces = sum(dot(part, rec_level) for part in split3(wave))
+        traces = dot(jnp.concatenate(split3(wave), axis=1), level3)
         cell = lax.broadcasted_iota(jnp.int32, (block, nrec), 0) + x0 * by
+        hit = cell == rec_code
+        hits[x0 * by : x0 * by + block, :] = hit.astype(F32).astype(BF16)
         picked = picked + jnp.sum(
-            jnp.where(cell == rec_code, traces, 0.0), axis=0, keepdims=True
+            jnp.where(hit, traces, 0.0), axis=0, keepdims=True
         )
     wave_out = pltpu.make_async_copy(prev, wave_o, osem.at[0])
     wave_out.start()
@@ -385,7 +394,9 @@
 
     wait_rims(adj_rims)
     rim_terms(1, acurl)
-    misfit_parts = split3(misfit)
+    misfit3 = jnp.concatenate(split3(rec_level * misfit), axis=1)
+
+    cas_side = jnp.concatenate([cas_z[nz * i : nz * (i + 1), :] for i in range(3)], axis=1)
 
     parts = bx // step_x
 
@@ -411,12 +422,8 @@
         for c in range(chunks)
     ]
     for x0 in range(0, bx, step_x):
-        cell = lax.broadcasted_iota(jnp.int32, (block, nrec), 0) + x0 * by
-        hit = cell == rec_code
-        added = sum(
-            dot(jnp.where(hit, part.astype(F32), 0.0).astype(BF16), rec_level, NT)
-            for part in misfit_parts
-        ).reshape(step_x, by, nz)
+        hit = hits[x0 * by : x0 * by + block, :]
+        added = dot(jnp.concatenate([hit] * 3, axis=1), misfit3, NT).reshape(step_x, by, nz)
         for x in range(x0, x0 + step_x):
             total = acurl[x]
             extra = x_rim(1, x)
@@ -428,9 +435,8 @@
             acurl[x] = grad
             anow[x] = grad * logs[x] - 1.0
 
-        high, low = split(acurl[x0 : x0 + step_x].reshape(block, nz))
-        zsend[:, x0 * by : x0 * by + block] = (
-            dot(cas_z[0], high, NT) + dot(cas_z[1], high, NT) + dot(cas_z[0], low, NT)
+        zsend[:, x0 * by : x0 * by + block] = dot(
+            cas_side, parts3(acurl[x0 : x0 + step_x].reshape(block, nz)), NT
         )
         part = x0 // step_x
         for copy in z_copies[0][part * (nyp - 1) : (part + 1) * (nyp - 1)]:
@@ -453,9 +459,7 @@
         return line_tab[0, gy, c * sub : (c + 1) * sub, :]
 
     def at(c, x):
-        first = (x // pair) * sub
-        left = (x % pair) * total_y
-        return lines[c, first : first + sub, left : left + total_y]
+        return lines[c, x * sub : (x + 1) * sub, :]
 
     def segment(o):
         return (
@@ -479,16 +483,15 @@
     def lateral(c):
         for copy in z_copies[c]:
             copy.wait_recv()
-        block = jnp.concatenate(
-            [
-                jnp.concatenate(
-                    [zrecv[c, p, :, LANES * j : LANES * (j + 1)] for p in range(nyp)], axis=1
-                )
-                for j in range(pairs)
-            ],
-            axis=0,
-        )
-        lines[c] = dot3(block, fwd_y)
+        rows_of = [[] for _ in range(bx)]
+        for j in range(pairs):
+            here = [zrecv[c, p, :, LANES * j : LANES * (j + 1)] for p in range(nyp)]
+            for p in range(0, nyp, 2):
+                first, second = trade(here[p], here[p + 1])
+                rows_of[2 * j].append(first)
+                rows_of[2 * j + 1].append(second)
+        block = jnp.concatenate([jnp.concatenate(row, axis=1) for row in rows_of], axis=0)
+        lines[c] = dot3(block, cas_y)
         r = ratio(c)
         up = at(c, 0)
         down = at(c, bx - 1)
@@ -557,12 +560,16 @@
             ahead = r * down
             here = at(c, x)
             down = here + ahead
-            first = (x // pair) * sub
-            left = (x % pair) * total_y
-            lines[c, first : first + sub, left : left + total_y] = gain * (ups[x] + ahead)
-        field = dot3(lines[c], inv_y)
-        for p in range(nyp):
-            isend[c, p] = field[:, LANES * p : LANES * (p + 1)]
+            lines[c, x * sub : (x + 1) * sub, :] = gain * (ups[x] + ahead)
+        out = dot3(lines[c], cas_y)
+        for j in range(pairs):
+            one = out[2 * j * sub : (2 * j + 1) * sub, :]
+            two = out[(2 * j + 1) * sub : (2 * j + 2) * sub, :]
+            for p in range(0, nyp, 2):
+                here = slice(p * by, (p + 2) * by)
+                first, second = trade(one[:, here], two[:, here])
+                isend[c, p, sub * j : sub * (j + 1), :] = first
+                isend[c, p + 1, sub * j : sub * (j + 1), :] = second
         copies = []
         for i in range(1, nyp):
             to = lax.rem(gy + i, nyp)
@@ -714,12 +721,13 @@
         pltpu.VMEM((2, 2, REACH * bx, nz), F32),
         pltpu.VMEM((nz, bx * by), F32),
         pltpu.VMEM((chunks, nyp, sub, bx * by), F32),
-        pltpu.VMEM((chunks, pairs * sub, nyp * LANES), F32),
+        pltpu.VMEM((chunks, bx * sub, total_y), F32),
         pltpu.VMEM((chunks, nyp, pairs * sub, LANES), F32),
         pltpu.VMEM((chunks, nxp, 2 * rows, LANES), F32),
         pltpu.VMEM((chunks, nxp, 2 * rows, LANES), F32),
         pltpu.VMEM((chunks, nxp, 2 * rows, LANES), F32),
         pltpu.VMEM((chunks, nxp, 2 * rows, LANES), F32),
+        pltpu.VMEM((bx * by, receivers.shape[0]), BF16),
         dma((7,)),
         dma((SMALL,)),
         dma((4,)),
@@ -751,7 +759,7 @@
         scratch_shapes=[
             whole,
             pltpu.VMEM(spread.shape, F32),
-            pltpu.VMEM((2, nz, nz), BF16),
+            pltpu.VMEM(small[7].shape, BF16),
             whole,
             pltpu.VMEM((3, bx, by, nz), F32),
             dma((6,)),

time: 47 us -> 40.1 us (0.85)
  Pallas kernels: 44.9 us -> 38 us
    pallas_call x1, Pallas kernels: 42 us -> 35.1 us  [per_device(): pl.pallas_call(functools.partial(kernel, nxp, nyp, chunks), out_shape=(fi...]
where the time goes in v5:
time: 40.1 us; the launch traced here: 39.9 us
  Pallas kernels  38 us (95%)
  between operations  1.93 us (5%)
    pallas_call x1, Pallas kernels, per_device(): pl.pallas_call(functools.partial(kernel, nxp, nyp, chunks), out_shape=(fi...  35.1 us
    pallas_call x1, Pallas kernels, per_device(): pl.pallas_call(finish, out_shape=(field,) * 4, in_specs=[anywhere] * 5 +...  2.91 us

profile of v5, /device:TPU:0, one launch (start us, length us, event | category | flops | bytes accessed | tf_op | source)
XLA Modules:
  0.0 39.9 jit_solution(6969829505256207996)
XLA Ops:
  1.9 35.1 %shard_map.201 = (f32[16,64,128]{2,1,0:T(8,128)}, f32[16,64,128]{2,1,0:T(8,128)}, f32[16,64,128]{2,1,0:T(8,128)}, f32[16,64,128]{2,1,0:T(8,128)}, f32[2,4,128,128]{3,2,1,0:T(8,128)}) custom-call(f32[16,64,128]{2,1,0:T(8,128)} %mean_h.1, f32[16,64,128]{2,1,0:T(8,128)} %scale_h.1, f32[16,64,128]{2,1,0:T(8,128)} %noise_h.1, f32[16,64,128]{2,1,0:T(8,128)} %prev_h.1, ...), custom_call_target="tpu_custom_call" | custom-call | tf_op jit(solution)/shard_map/pallas_call | solution.py:742
  37.0 2.9 %shard_map.202 = (f32[16,64,128]{2,1,0:T(8,128)}, f32[16,64,128]{2,1,0:T(8,128)}, f32[16,64,128]{2,1,0:T(8,128)}, f32[16,64,128]{2,1,0:T(8,128)}) custom-call(f32[16,64,128]{2,1,0:T(8,128)} %get-tuple-element.9.wave, f32[16,64,128]{2,1,0:T(8,128)} %get-tuple-element.10.adjoint, f32[16,64,128]{2,1,0:T(8,128)} %get-tuple-element.11.sample_h, ...), custom_call_target="tpu_custom_call" | custom-call | tf_op jit(solution)/shard_map/pallas_call | solution.py:754

commit v6 on v5

--- a/solution.py
+++ b/solution.py
@@ -33,6 +33,16 @@
     high = table.astype(ml_dtypes.bfloat16)
     low = (table - high.astype(np.float64)).astype(ml_dtypes.bfloat16)
     return np.concatenate([high, low, high])
+
+
+def thirds(table):
+    parts = []
+    for _ in range(3):
+        part = table.astype(ml_dtypes.bfloat16)
+        table = table - part.astype(np.float64)
+        parts.append(part)
+    high, mid, low = parts
+    return np.concatenate([high, mid, low, high, mid, high])
 
 
 def cas(length):
@@ -75,7 +85,7 @@
     segment = segment.transpose(1, 2, 3, 5, 0, 4, 6).reshape(nyp, chunks, nxp, 2, rows, LANES)
     as32 = lambda a: np.ascontiguousarray(a).astype(np.float32)
     return (
-        as32(along_z),
+        thirds(along_z),
         as32(faces),
         halves(cas(nz)),
         halves(cas(total_y)),
@@ -98,6 +108,11 @@
 
 def dot(a, b, dims=NN):
     return lax.dot_general(a, b, dims, preferred_element_type=F32)
+
+
+def parts6(x):
+    high, mid, low = split3(x)
+    return jnp.concatenate([high, high, high, mid, mid, low], axis=1)
 
 
 def parts3(x):
@@ -272,6 +287,29 @@
 
     loads[0].wait()
     pack_faces(0, wpad)
+    small_loads[0].wait()
+    small_loads[1].wait()
+
+    def codes(points):
+        across = points[0:1, :] - gx * bx
+        lateral = points[1:2, :] - gy * by
+        inside = (across >= 0) & (across < bx) & (lateral >= 0) & (lateral < by)
+        return jnp.where(inside, across * by + lateral, -1)
+
+    src_code = codes(src_row)
+    rec_code = codes(rec_row)
+
+    nsrc, nrec = src_row.shape[1], rec_row.shape[1]
+    src_level = lax.broadcasted_iota(jnp.int32, (nz, nsrc), 0) == src_row[2:3, :]
+    src_level = src_level.astype(F32).astype(BF16)
+    rec_level = lax.broadcasted_iota(jnp.int32, (nz, nrec), 0) == rec_row[2:3, :]
+    rec_level = rec_level.astype(F32)
+    level3 = jnp.concatenate([rec_level.astype(BF16)] * 3, axis=0)
+    step_x = 4
+    block = step_x * by
+    for x0 in range(0, bx, step_x):
+        cell = lax.broadcasted_iota(jnp.int32, (block, nrec), 0) + x0 * by
+        hits[x0 * by : x0 * by + block, :] = (cell == rec_code).astype(F32).astype(BF16)
 
     for load in loads[1:5]:
         load.wait()
@@ -298,7 +336,7 @@
     def inner_laplacian(padded, out):
         for x0 in range(0, bx, REACH):
             block = padded[x0 : x0 + REACH, PAD : PAD + by, :].reshape(REACH * by, nz)
-            depthwise = exact(block, along_z[...]).reshape(REACH, by, nz)
+            depthwise = dot(parts6(block), along_z[...]).reshape(REACH, by, nz)
             for x in range(x0, x0 + REACH):
                 total = depthwise[x - x0] + 3.0 * STENCIL_WEIGHTS[0] * padded[x, centre, :]
                 for o in range(1, REACH + 1):
@@ -310,18 +348,9 @@
                     total = total + STENCIL_WEIGHTS[o] * near
                 out[x] = total
 
-    for load in small_loads:
+    for load in small_loads[2:]:
         load.wait()
     inner_laplacian(wpad, curl)
-
-    def codes(points):
-        across = points[0:1, :] - gx * bx
-        lateral = points[1:2, :] - gy * by
-        inside = (across >= 0) & (across < bx) & (lateral >= 0) & (lateral < by)
-        return jnp.where(inside, across * by + lateral, -1)
-
-    src_code = codes(src_row)
-    rec_code = codes(rec_row)
 
     def rim_terms(field, out):
         for side in range(2):
@@ -367,14 +396,6 @@
 
     moment = (step[...] - NSTEPS // 2).astype(F32) * (math.pi * PULSE_FREQUENCY)
     pulse = PULSE_AMPLITUDE * (1.0 - 2.0 * moment * moment) * jnp.exp(-moment * moment)
-    nsrc, nrec = src_row.shape[1], rec_row.shape[1]
-    src_level = lax.broadcasted_iota(jnp.int32, (nz, nsrc), 0) == src_row[2:3, :]
-    src_level = src_level.astype(F32).astype(BF16)
-    rec_level = lax.broadcasted_iota(jnp.int32, (nz, nrec), 0) == rec_row[2:3, :]
-    rec_level = rec_level.astype(F32)
-    level3 = jnp.concatenate([rec_level.astype(BF16)] * 3, axis=0)
-    step_x = 4
-    block = step_x * by
     picked = jnp.zeros((1, nrec), F32)
     for x0 in range(0, bx, step_x):
         cell = lax.broadcasted_iota(jnp.int32, (block, nsrc), 0) + x0 * by
@@ -382,11 +403,9 @@
         wave = prev[x0 : x0 + step_x].reshape(block, nz) + pulse * dot(hit, src_level, NT)
         prev[x0 : x0 + step_x] = wave.reshape(step_x, by, nz)
         traces = dot(jnp.concatenate(split3(wave), axis=1), level3)
-        cell = lax.broadcasted_iota(jnp.int32, (block, nrec), 0) + x0 * by
-        hit = cell == rec_code
-        hits[x0 * by : x0 * by + block, :] = hit.astype(F32).astype(BF16)
+        hit = hits[x0 * by : x0 * by + block, :].astype(F32)
         picked = picked + jnp.sum(
-            jnp.where(hit, traces, 0.0), axis=0, keepdims=True
+            hit * traces, axis=0, keepdims=True
         )
     wave_out = pltpu.make_async_copy(prev, wave_o, osem.at[0])
     wave_out.start()
@@ -433,7 +452,6 @@
             anext[x] = adjoint
             grad = (2.0 * VELOCITY_GAIN) * speed[x] * adjoint * curl[x]
             acurl[x] = grad
-            anow[x] = grad * logs[x] - 1.0
 
         zsend[:, x0 * by : x0 * by + block] = dot(
             cas_side, parts3(acurl[x0 : x0 + step_x].reshape(block, nz)), NT
@@ -448,6 +466,8 @@
 
     adj_out = pltpu.make_async_copy(anext, adj_o, osem.at[1])
     adj_out.start()
+    for x in range(bx):
+        anow[x] = acurl[x] * logs[x] - 1.0
     lgrad_out = pltpu.make_async_copy(anow, lgrad_o, osem.at[2])
     lgrad_out.start()
     sample_out = pltpu.make_async_copy(mean, sample_o, osem.at[3])
@@ -651,14 +671,9 @@
         pltpu.make_async_copy(adjoint, kept.at[1], sem.at[4]),
         pltpu.make_async_copy(lgrad, kept.at[2], sem.at[5]),
     ]
-    for copy in copies[3:] + copies[:3]:
+    for copy in copies:
         copy.start()
     outs = []
-    for i, kept_o in enumerate((wave_o, adj_o, lgrad_o)):
-        copies[3 + i].wait()
-        out = pltpu.make_async_copy(kept.at[i], kept_o, out_sem.at[pairs + i])
-        out.start()
-        outs.append(out)
     for copy in copies[:3]:
         copy.wait()
     for j in range(pairs):
@@ -672,6 +687,13 @@
         out = pltpu.make_async_copy(search.at[here], search_o.at[here], out_sem.at[j])
         out.start()
         outs.append(out)
+        if j < 3:
+            copies[3 + j].wait()
+            out = pltpu.make_async_copy(
+                kept.at[j], (wave_o, adj_o, lgrad_o)[j], out_sem.at[pairs + j]
+            )
+            out.start()
+            outs.append(out)
     for out in outs:
         out.wait()
 

time: 40.1 us -> 40.2 us (level)
  no operation moved by 1% of the time
where the time goes in v6:
time: 40.2 us; the launch traced here: 40 us
  Pallas kernels  38.1 us (95%)
  between operations  1.93 us (5%)
    pallas_call x1, Pallas kernels, per_device(): pl.pallas_call(functools.partial(kernel, nxp, nyp, chunks), out_shape=(fi...  35.1 us
    pallas_call x1, Pallas kernels, per_device(): pl.pallas_call(finish, out_shape=(field,) * 4, in_specs=[anywhere] * 5 +...  3.04 us

profile of v6, /device:TPU:0, one launch (start us, length us, event | category | flops | bytes accessed | tf_op | source)
XLA Modules:
  0.0 40.0 jit_solution(11846964243364761865)
XLA Ops:
  1.9 35.1 %shard_map.201 = (f32[16,64,128]{2,1,0:T(8,128)}, f32[16,64,128]{2,1,0:T(8,128)}, f32[16,64,128]{2,1,0:T(8,128)}, f32[16,64,128]{2,1,0:T(8,128)}, f32[2,4,128,128]{3,2,1,0:T(8,128)}) custom-call(f32[16,64,128]{2,1,0:T(8,128)} %mean_h.1, f32[16,64,128]{2,1,0:T(8,128)} %scale_h.1, f32[16,64,128]{2,1,0:T(8,128)} %noise_h.1, f32[16,64,128]{2,1,0:T(8,128)} %prev_h.1, ...), custom_call_target="tpu_custom_call" | custom-call | tf_op jit(solution)/shard_map/pallas_call | solution.py:764
  37.0 3.0 %shard_map.202 = (f32[16,64,128]{2,1,0:T(8,128)}, f32[16,64,128]{2,1,0:T(8,128)}, f32[16,64,128]{2,1,0:T(8,128)}, f32[16,64,128]{2,1,0:T(8,128)}) custom-call(f32[16,64,128]{2,1,0:T(8,128)} %get-tuple-element.9.wave, f32[16,64,128]{2,1,0:T(8,128)} %get-tuple-element.10.adjoint, f32[16,64,128]{2,1,0:T(8,128)} %get-tuple-element.11.sample_h, ...), custom_call_target="tpu_custom_call" | custom-call | tf_op jit(solution)/shard_map/pallas_call | solution.py:776

commit v7 on v6

--- a/solution.py
+++ b/solution.py
@@ -610,13 +610,9 @@
         own_fields.append(own)
         v_copies.append(copies)
 
-    for stage in range(chunks + 2):
-        if stage >= 2:
-            back(stage - 2)
-        if 1 <= stage <= chunks:
-            close(stage - 1)
-        if stage < chunks:
-            lateral(stage)
+    for stage in (lateral, close, back):
+        for c in range(chunks):
+            stage(c)
 
     for c in range(chunks):
         for copy in v_copies[c]:

time: 40.2 us -> 39.6 us (0.985)
  Pallas kernels: 38.1 us -> 37.5 us
    pallas_call x1, Pallas kernels: 35.1 us -> 34.5 us  [per_device(): pl.pallas_call(functools.partial(kernel, nxp, nyp, chunks), out_shape=(fi...]
where the time goes in v7:
time: 39.6 us; the launch traced here: 39.4 us
  Pallas kernels  37.5 us (95%)
  between operations  1.93 us (5%)
    pallas_call x1, Pallas kernels, per_device(): pl.pallas_call(functools.partial(kernel, nxp, nyp, chunks), out_shape=(fi...  34.5 us
    pallas_call x1, Pallas kernels, per_device(): pl.pallas_call(finish, out_shape=(field,) * 4, in_specs=[anywhere] * 5 +...  3.06 us

profile of v7, /device:TPU:0, one launch (start us, length us, event | category | flops | bytes accessed | tf_op | source)
XLA Modules:
  0.0 39.4 jit_solution(15079027171464167603)
XLA Ops:
  1.9 34.5 %shard_map.201 = (f32[16,64,128]{2,1,0:T(8,128)}, f32[16,64,128]{2,1,0:T(8,128)}, f32[16,64,128]{2,1,0:T(8,128)}, f32[16,64,128]{2,1,0:T(8,128)}, f32[2,4,128,128]{3,2,1,0:T(8,128)}) custom-call(f32[16,64,128]{2,1,0:T(8,128)} %mean_h.1, f32[16,64,128]{2,1,0:T(8,128)} %scale_h.1, f32[16,64,128]{2,1,0:T(8,128)} %noise_h.1, f32[16,64,128]{2,1,0:T(8,128)} %prev_h.1, ...), custom_call_target="tpu_custom_call" | custom-call | tf_op jit(solution)/shard_map/pallas_call | solution.py:760
  36.4 3.1 %shard_map.202 = (f32[16,64,128]{2,1,0:T(8,128)}, f32[16,64,128]{2,1,0:T(8,128)}, f32[16,64,128]{2,1,0:T(8,128)}, f32[16,64,128]{2,1,0:T(8,128)}) custom-call(f32[16,64,128]{2,1,0:T(8,128)} %get-tuple-element.9.wave, f32[16,64,128]{2,1,0:T(8,128)} %get-tuple-element.10.adjoint, f32[16,64,128]{2,1,0:T(8,128)} %get-tuple-element.11.sample_h, ...), custom_call_target="tpu_custom_call" | custom-call | tf_op jit(solution)/shard_map/pallas_call | solution.py:772
